TPU v7x, 128 devices: a whole 4x4x4 slice. The times are simulated.
128 devices in a mesh: dp: 32 (over y, z, core), tp: 4 (over x).
Axes of the slice: x: 4, y: 4, z: 4, core: 2. Of those that a mesh axis runs over, the one named last changes fastest.
Arguments:
- query: bfloat16 [1024, 64, 576], P('dp', 'tp'), may hold values from -30 to 30
- cache_pool: bfloat16 [4096, 64, 576], P('dp'), may hold values from -6 to 6
- block_scale: bfloat16 [4096], P('dp'), may hold values from 0.25 to 2.5
- block_table: int32 [1024, 4], P('dp'), may hold values from 0 to 127, as said below
- lengths: int32 [1024], P('dp'), may hold values from 2 to 256, as said below
- migration: int32 [16, 3], replicated, may hold values from 0 to 1023, as said below
- value_up: bfloat16 [64, 512, 128], P('tp'), may hold values from -0.25 to 0.25
- out_weight: bfloat16 [8192, 7168], P('tp', 'dp'), may hold values from -0.0625 to 0.0625
- residual: bfloat16 [1024, 7168], P(('dp', 'tp')), may hold values from -6 to 6
- norm_gain: float32 [7168], replicated, may hold values from 0.1 to 1.9
- expert_ids: int32 [1024, 8], P(('dp', 'tp')), may hold values from 0 to 31, all different within a row; in each aligned block of 8 rows (0 to 7, 8 to 15, ...) at most 4 rows name the same one
- gate_weights: float32 [1024, 8], P(('dp', 'tp')), may hold values from 0.2 to 0.8
- expert_owner: int32 [32], replicated, may hold values from 0 to 31, each once
- w_gate: bfloat16 [32, 7168, 1024], P('dp', None, 'tp'), may hold values from -0.0625 to 0.0625
- w_up: bfloat16 [32, 7168, 1024], P('dp', None, 'tp'), may hold values from -0.0625 to 0.0625
- w_down: bfloat16 [32, 1024, 7168], P('dp', 'tp'), may hold values from -0.1875 to 0.1875
Outputs:
- mixed: bfloat16 [1024, 7168], P(('dp', 'tp'))
- arrived_blocks: bfloat16 [32, 4, 64, 576], P('dp')
- arrived_scales: bfloat16 [32, 4], P('dp')
Inputs may be any that keep to these rules, and one draw needn't show every extreme that they name: `block_table`: per data rank, its 32 requests' rows together name each of its 128 local block numbers exactly once. `lengths`: some request has exactly 256 positions. `migration`: each rank is a source at most once and a destination at most once, never both; the request lives on its source rank (request // 32 equals the source); request 1024 - 1 migrates in every draw. `expert_ids`: in the rows of one device no expert is named more than 4 times.
All inputs are finite; a program needn't handle non-finite values.
Results may differ from a plain program's by a relative error of at most 0.018.
Values may be sent and summed in bfloat16 or wider, within the bound.
A program may use at most 192 MiB of HBM per device.

v0:
```python
import jax
import jax.numpy as jnp
from jax import lax
from jax.sharding import PartitionSpec as P

softmax_scale = 192.0 ** (-0.5)
norm_eps = 1e-06


def attend(query, cache_pool, block_scale, block_table, lengths, value_up):
    requests = block_table.shape[0]
    block_size = cache_pool.shape[1]
    latent = value_up.shape[1]
    context = block_table.shape[1] * block_size
    tiles = cache_pool[block_table].reshape(requests, context, cache_pool.shape[2])
    pos_scale = jnp.repeat(block_scale[block_table].astype(jnp.float32), block_size, axis=1)
    scores = jnp.einsum("rhc,rpc->rhp", query, tiles, preferred_element_type=jnp.float32)
    scores = scores * softmax_scale * pos_scale[:, None, :]
    live = jnp.arange(context)[None, :] < lengths[:, None]
    scores = jnp.where(live[:, None, :], scores, -1e30)
    top = jnp.max(scores, axis=2, keepdims=True)
    expo = jnp.exp(scores - top)
    weight = expo / jnp.sum(expo, axis=2, keepdims=True)
    coef = (weight * pos_scale[:, None, :]).astype(jnp.bfloat16)
    latent_out = jnp.einsum(
        "rhp,rpc->rhc", coef, tiles[:, :, :latent], preferred_element_type=jnp.float32
    ).astype(jnp.bfloat16)
    head_out = jnp.einsum(
        "rhc,hcv->rhv", latent_out, value_up, preferred_element_type=jnp.float32
    ).astype(jnp.bfloat16)
    return head_out.reshape(requests, -1)


def body(
    query,
    cache_pool,
    block_scale,
    block_table,
    lengths,
    migration,
    value_up,
    out_weight,
    residual,
    norm_gain,
    expert_ids,
    gate_weights,
    expert_owner,
    w_gate,
    w_up,
    w_down,
):
    ranks = lax.axis_size("dp")
    groups = lax.axis_size("tp")
    rank = lax.axis_index("dp")
    requests = block_table.shape[0]
    width = residual.shape[1]
    leaving = migration[:, 1] == rank
    local_req = jnp.sum(jnp.where(leaving, migration[:, 0] - rank * requests, 0))
    is_source = jnp.any(leaving)
    out_rows = lax.dynamic_index_in_dim(block_table, local_req, 0, keepdims=False)
    out_blocks = jnp.where(is_source, cache_pool[out_rows], 0)[None]
    out_scales = jnp.where(is_source, block_scale[out_rows], 0)[None]
    coming = migration[:, 2] == rank
    sender = jnp.sum(jnp.where(coming, migration[:, 1], 0))
    has_in = jnp.any(coming)
    empty = (
        jnp.zeros(out_blocks.shape[1:], jnp.bfloat16),
        jnp.zeros(out_scales.shape[1:], jnp.bfloat16),
    )
    blocks = lax.all_gather(out_blocks, "dp", axis=0, tiled=True)
    scales = lax.all_gather(out_scales, "dp", axis=0, tiled=True)
    inside = has_in & (sender >= 0) & (sender < blocks.shape[0])
    chosen = jnp.clip(sender, 0, blocks.shape[0] - 1)
    pick_blocks = lax.dynamic_index_in_dim(blocks, chosen, 0, keepdims=False)
    pick_scales = lax.dynamic_index_in_dim(scales, chosen, 0, keepdims=False)
    arrived_blocks = jnp.where(inside, pick_blocks, empty[0])
    arrived_scales = jnp.where(inside, pick_scales, empty[1])
    head_out = attend(query, cache_pool, block_scale, block_table, lengths, value_up)
    columns = out_weight.shape[1]
    partial_value = jnp.dot(
        lax.all_gather(head_out, "dp", axis=0, tiled=True),
        out_weight,
        preferred_element_type=jnp.float32,
    )
    summed = lax.psum_scatter(
        partial_value.reshape(ranks, requests, columns).astype(jnp.bfloat16),
        "tp",
        scatter_dimension=1,
        tiled=True,
    )
    landed = lax.all_to_all(summed, "dp", split_axis=0, concat_axis=2, tiled=True)
    proj = landed.reshape(landed.shape[1], landed.shape[2])
    stream = residual.astype(jnp.float32) + proj.astype(jnp.float32)
    power = jnp.mean(stream * stream, axis=1, keepdims=True)
    normed = (stream * lax.rsqrt(power + norm_eps) * norm_gain[None, :]).astype(jnp.bfloat16)
    tokens = normed.shape[0]
    topk = expert_ids.shape[1]
    experts = expert_owner.shape[0]
    capacity = min(tokens, max(2, 2 * tokens * topk // experts))
    picks = expert_ids[:, :, None] == jnp.arange(experts)[None, None, :]
    named = jnp.sum(picks, axis=1)
    before = jnp.cumsum(named, axis=0) - named
    slots = jnp.sum(jnp.where(picks, before[:, None, :], 0), axis=2)
    owners = jnp.sum(jnp.where(picks, expert_owner[None, None, :], 0), axis=2)
    target = owners * capacity + slots
    lanes = jnp.arange(ranks * capacity)
    hits = lanes[:, None, None] == target[None, :, :]
    placing = jnp.any(hits, axis=2).astype(jnp.bfloat16)
    combine = jnp.transpose(jnp.sum(jnp.where(hits, gate_weights[None, :, :], 0.0), axis=2))
    outgoing = (
        jnp.dot(placing, normed, preferred_element_type=jnp.float32)
        .astype(jnp.bfloat16)
        .reshape(ranks, capacity, width)
    )
    copies = jnp.broadcast_to(outgoing[:, None], (ranks, groups, capacity, width)).reshape(
        ranks * groups, capacity, width
    )
    rows = lax.all_to_all(copies, ("dp", "tp"), split_axis=0, concat_axis=0, tiled=True)
    flat = rows.reshape(-1, width)
    gate = jnp.dot(flat, w_gate[0], preferred_element_type=jnp.float32)
    upper = jnp.dot(flat, w_up[0], preferred_element_type=jnp.float32)
    hidden = (jax.nn.silu(gate) * upper).astype(jnp.bfloat16)
    returned = lax.all_to_all(
        jnp.dot(hidden, w_down[0], preferred_element_type=jnp.float32)
        .astype(jnp.bfloat16)
        .reshape(rows.shape),
        ("dp", "tp"),
        split_axis=0,
        concat_axis=0,
        tiled=True,
    )
    results = jnp.sum(returned.reshape(ranks, groups, capacity, width).astype(jnp.float32), axis=1)
    flat_results = results.reshape(ranks * capacity, width)
    moe = jnp.dot(combine, flat_results, precision=lax.Precision.HIGHEST)
    mixed = (stream + moe).astype(jnp.bfloat16)
    return (mixed, arrived_blocks[None], arrived_scales[None])


def solution(mesh):
    return jax.shard_map(
        body,
        mesh=mesh,
        in_specs=(
            P("dp", "tp", None),
            P("dp", None, None),
            P("dp"),
            P("dp", None),
            P("dp"),
            P(),
            P("tp", None, None),
            P("tp", "dp"),
            P(("dp", "tp"), None),
            P(),
            P(("dp", "tp"), None),
            P(("dp", "tp"), None),
            P(),
            P("dp", None, "tp"),
            P("dp", None, "tp"),
            P("dp", "tp", None),
        ),
        out_specs=(P(("dp", "tp"), None), P("dp", None, None, None), P("dp", None)),
        check_vma=False,
    )
```

profile of v0, /device:TPU:1, one launch (start us, length us, event | category | flops | bytes accessed | tf_op | source)
XLA Modules:
  0.0 486.6 jit_solution(6253931075473157532)
XLA Ops:
  7.2 0.0 all-gather.5.cloned.1.call-start
  7.2 0.8 compare_select_fusion
  8.1 0.7 iota_compare_fusion.2
  8.8 0.1 copy.37
  8.9 0.1 reshape.152
  9.0 1.6 gather_fusion.1
  10.6 0.1 reshape.189
  10.7 0.1 broadcast_in_dim.100
  10.8 0.1 mul.64
  10.9 14.8 %copy.38 = bf16[128,64,576]{2,1,0:T(8,128)(2,1)} copy(bf16[128,64,576]{0,2,1:T(8,128)(2,1)} %param.17) | data formatting | bytes 18874368 | tf_op args[1]
  25.7 11.8 %gather_fusion = bf16[128,64,576]{2,1,0:T(8,128)(2,1)} fusion(bf16[128,64,576]{2,1,0:T(8,128)(2,1)} %copy.38, s32[1024]{0:T(1024)S(1)} %pad_clamp_fusion.1), kind=kCustom, calls=%fused_computation | custom fusion | bytes 18874880 | tf_op jit(solution)/shard_map/gather | solution.py:15
  37.5 7.0 %fusion.36 = (f32[32,16]{1,0:T(8,128)S(1)}, f32[32,16,256]{2,1,0:T(8,128)S(1)}) fusion(bf16[32,256,576]{2,1,0:T(8,128)(2,1)} %bitcast.58, bf16[32,16,576]{2,1,0:T(8,128)(2,1)S(1)} %copy-done.4, f32[32,256]{1,0:T(8,128)S(1)} %broadcast_multiply_fusion, pred[32,256]{1,0:T(8,128)(4,1)S(1)} %iota_compare_fusion.2), kind=kOutput, calls=%fused_computation.70 | convolution fusion | flops 151519488 | bytes 10594304 | tf_op jit(solution)/shard_map/sub | solution.py:22
  44.4 4.6 fusion.9
  49.1 0.0 copy-start.7
  49.1 0.7 fusion.22
  49.8 0.7 copy.54
  50.5 0.0 all-gather.5.cloned.1.call-update
  50.5 0.0 reduce-scatter.4.cloned.1.call-start
  50.5 50.2 %all-gather.5.cloned.1.call-done = bf16[1024,2048]{1,0:T(8,128)(2,1)} async-done(((bf16[32,2048]{1,0:T(8,128)(2,1)}), bf16[1024,2048]{1,0:T(8,128)(2,1)}) %all-gather.5.cloned.1.call-update) | async-done | bytes 4194320 | tf_op jit(solution)/shard_map/all_gather | solution.py:81
  100.7 3.9 convolution_convert_fusion.2
  104.6 0.2 copy.42
  104.8 0.3 copy.53
  105.1 1.6 reshape.195
  106.7 0.0 reduce-scatter.4.cloned.1.call-update
  106.7 0.0 all-gather.7.cloned.1.call-start
  106.8 0.6 fusion.32
  109.4 0.2 dynamic-slice_reduce_fusion
  109.6 4.6 gather_fusion.2
  114.2 0.7 compare_reduce_fusion.1
  114.9 1.4 broadcast_select_fusion
  116.3 0.0 all-gather.7.cloned.1.call-update
  116.3 0.1 convert_reduce_fusion.1
  116.5 0.4 select_reduce_fusion.2
  116.9 8.3 %reduce-scatter.4.cloned.1.call-done = bf16[8,7168]{1,0:T(8,128)(2,1)} async-done(((bf16[32,7168]{1,0:T(8,128)(2,1)}), bf16[8,7168]{1,0:T(8,128)(2,1)}) %reduce-scatter.4.cloned.1.call-update) | async-done | bytes 114704
  125.2 1.1 reshape.196
  126.3 0.7 copy.47
  127.0 9.3 %all-to-all-start = ((bf16[32,8,224]{2,1,0:T(8,128)(2,1)}), bf16[32,8,224]{2,1,0:T(8,128)(2,1)S(1)}, u32[]{:S(2)}, u32[]{:S(2)}) async-start(bf16[32,8,224]{2,1,0:T(8,128)(2,1)} %copy.47), calls=%async_computation | async-start | bytes 262144 | tf_op jit(solution)/shard_map/all_to_all | solution.py:91
  136.3 0.1 fusion.31
  136.4 7.7 %all-to-all-done = bf16[32,8,224]{2,1,0:T(8,128)(2,1)S(1)} async-done(((bf16[32,8,224]{2,1,0:T(8,128)(2,1)}), bf16[32,8,224]{2,1,0:T(8,128)(2,1)S(1)}, u32[]{:S(2)}, u32[]{:S(2)}) %all-to-all-start) | async-done | bytes 114720 | tf_op jit(solution)/shard_map/all_to_all | solution.py:91
  144.1 0.1 copy.43
  144.2 0.2 reshape.147
  144.4 0.2 multiply_reduce_fusion
  144.6 0.7 convolution_convert_fusion.1
  145.3 1.6 broadcast_in_dim.107
  146.9 6.7 %broadcast_in_dim.108 = bf16[32,4,4,7168]{3,2,1,0:T(4,128)(2,1)} broadcast(bf16[32,4,7168]{2,1,0:T(4,128)(2,1)} %broadcast_in_dim.107), dimensions={0,2,3} | broadcast | bytes 9175040 | tf_op jit(solution)/shard_map/broadcast_in_dim | solution.py:115
  153.7 105.3 %all_to_all.19 = bf16[128,4,7168]{2,1,0:T(4,128)(2,1)} all-to-all(bf16[128,4,7168]{2,1,0:T(4,128)(2,1)} %bitcast.60), channel_id=1, replica_groups=mesh['dp'=32,'tp'=4] {'dp','tp'}, dimensions={0} | all-to-all | bytes 14680064 | tf_op jit(solution)/shard_map/all_to_all | solution.py:118
  259.0 12.1 %reshape.144 = bf16[512,7168]{1,0:T(8,128)(2,1)} reshape(bf16[128,4,7168]{2,1,0:T(4,128)(2,1)} %all_to_all.19) | data formatting | bytes 14680064 | tf_op jit(solution)/shard_map/reshape | solution.py:119
  271.1 6.2 %fusion.7 = f32[512,256]{1,0:T(8,128)S(1)} fusion(bf16[512,7168]{1,0:T(8,128)(2,1)} %reshape.144, bf16[1,7168,256]{2,1,0:T(8,128)(2,1)} %param.29), kind=kOutput, calls=%fused_computation.15 | convolution fusion | flops 1879048192 | bytes 11534336 | tf_op jit(solution)/shard_map/dot_general | solution.py:120
  277.3 16.0 %convolution_convert_fusion = bf16[512,7168]{1,0:T(8,128)(2,1)} fusion(bf16[1,256,7168]{2,1,0:T(8,128)(2,1)} %param.31, bf16[512,7168]{1,0:T(8,128)(2,1)} %reshape.144, bf16[1,7168,256]{2,1,0:T(8,128)(2,1)} %param.30, f32[512,256]{1,0:T(8,128)S(1)} %fusion.7), kind=kOutput, calls=%fused_computation.6 | convolution fusion | flops 3762552832 | bytes 22544384 | tf_op jit(solution)/shard_map/dot_general | solution.py:124
  293.3 12.6 %reshape.145 = bf16[128,4,7168]{2,1,0:T(4,128)(2,1)} reshape(bf16[512,7168]{1,0:T(8,128)(2,1)} %convolution_convert_fusion) | data formatting | bytes 14680064 | tf_op jit(solution)/shard_map/reshape | solution.py:126
  306.0 9.7 %all-to-all-start.2 = ((bf16[128,4,7168]{2,1,0:T(4,128)(2,1)}), bf16[128,4,7168]{2,1,0:T(4,128)(2,1)}, u32[]{:S(2)}, u32[]{:S(2)}) async-start(bf16[128,4,7168]{2,1,0:T(4,128)(2,1)} %reshape.145), calls=%async_computation.2 | async-start | bytes 14680064 | tf_op jit(solution)/shard_map/all_to_all | solution.py:123
  317.6 0.6 gather_fusion.3
  318.3 0.6 dynamic-slice
  319.5 0.6 broadcast_select_fusion.1
  320.1 0.2 dynamic-update-slice
  320.4 0.1 reshape.183
  321.2 137.1 %all-reduce.1 = bf16[32,4]{1,0:T(8,128)(2,1)S(1)} all-reduce(bf16[32,4]{1,0:T(8,128)(2,1)S(1)} %reshape.183), channel_id=3, replica_groups=mesh['dp'=32,'tp'=4] {'dp'}, use_global_device_ids=true, to_apply=%add | all-reduce | flops 128 | bytes 512
  458.3 0.5 broadcast_select_fusion.2
  458.8 0.1 select_reduce_fusion
  458.9 0.0 all-gather.7.cloned.1.call-done
  458.9 1.7 dynamic-slice_select_fusion
  460.7 9.6 %convert_reduce_fusion = f32[32,4,7168]{2,1,0:T(4,128)} fusion(bf16[128,4,7168]{2,1,0:T(4,128)(2,1)} %all-to-all-done.2), kind=kLoop, calls=%fused_computation.5 | loop fusion | flops 6422528 | bytes 11010048 | tf_op jit(solution)/shard_map/reduce_sum | solution.py:132
  470.3 5.3 %reshape.146 = f32[128,7168]{1,0:T(8,128)} reshape(f32[32,4,7168]{2,1,0:T(4,128)} %convert_reduce_fusion) | data formatting | bytes 7340032 | tf_op jit(solution)/shard_map/reshape | solution.py:133
  475.6 4.5 fusion.3
  (34 shorter events, 0.2 us)
Async XLA Ops:
  7.2 41.9 %copy-start = (bf16[16,512,128]{2,1,0:T(8,128)(2,1)S(1)}, bf16[16,512,128]{2,1,0:T(8,128)(2,1)}, u32[]{:S(2)}) copy-start(bf16[16,512,128]{2,1,0:T(8,128)(2,1)} %param.22) | copy-start | bytes 6291460
  7.2 93.5 %all-gather.5.cloned.1.call-start = ((), (), s32[]{:S(2)}) async-start(), calls=%async_computation.4 | async-start | bytes 4325376 | tf_op jit(solution)/shard_map/all_gather | solution.py:81
  25.7 11.8 %copy-start.4 = (bf16[32,16,576]{2,1,0:T(8,128)(2,1)S(1)}, bf16[32,16,576]{2,1,0:T(8,128)(2,1)}, u32[]{:S(2)}) copy-start(bf16[32,16,576]{2,1,0:T(8,128)(2,1)} %param.16) | copy-start | bytes 1769476
  49.0 57.7 %copy-start.9 = (s32[16,3]{0,1:T(4,128)S(1)}, s32[16,3]{0,1:T(4,128)}, u32[]{:S(2)}) copy-start(s32[16,3]{0,1:T(4,128)} %param.21) | copy-start | bytes 580
  49.1 60.3 %copy-start.7 = (s32[32,4]{0,1:T(4,128)S(1)}, s32[32,4]{0,1:T(4,128)}, u32[]{:S(2)}) copy-start(s32[32,4]{0,1:T(4,128)} %param.19) | copy-start | bytes 1540
  49.1 67.2 %copy-start.6 = (s32[8,8]{1,0:T(8,128)S(1)}, s32[8,8]{1,0:T(8,128)}, u32[]{:S(2)}) copy-start(s32[8,8]{1,0:T(8,128)} %param.26) | copy-start | bytes 772
  49.1 67.4 %copy-start.10 = (s32[32]{0:T(128)S(1)}, s32[32]{0:T(128)}, u32[]{:S(2)}) copy-start(s32[32]{0:T(128)} %param.28) | copy-start | bytes 388
  49.8 94.6 %copy-start.3 = (bf16[8,7168]{1,0:T(8,128)(2,1)S(1)}, bf16[8,7168]{1,0:T(8,128)(2,1)}, u32[]{:S(2)}) copy-start(bf16[8,7168]{1,0:T(8,128)(2,1)} %param.24) | copy-start | bytes 344068
  50.5 94.1 %copy-start.5 = (f32[7168]{0:T(1024)S(1)}, f32[7168]{0:T(1024)}, u32[]{:S(2)}) copy-start(f32[7168]{0:T(1024)} %param.25) | copy-start | bytes 86020
  50.5 74.7 %reduce-scatter.4.cloned.1.call-start = ((), (), s32[]{:S(2)}) async-start(), calls=%async_computation.6 | async-start | bytes 573440
  106.7 352.2 %all-gather.7.cloned.1.call-start = ((), (), s32[]{:S(2)}) async-start(), calls=%async_computation.5 | async-start | bytes 10813440 | tf_op jit(solution)/shard_map/all_gather | solution.py:70
  127.0 17.1 %all-to-all-start = ((bf16[32,8,224]{2,1,0:T(8,128)(2,1)}), bf16[32,8,224]{2,1,0:T(8,128)(2,1)S(1)}, u32[]{:S(2)}, u32[]{:S(2)}) async-start(bf16[32,8,224]{2,1,0:T(8,128)(2,1)} %copy.47), calls=%async_computation | async-start | bytes 262144 | tf_op jit(solution)/shard_map/all_to_all | solution.py:91
  306.0 11.6 %copy-start.2 = (bf16[128]{0:T(256)(128)(2,1)S(1)}, bf16[128]{0:T(256)(128)(2,1)}, u32[]{:S(2)}) copy-start(bf16[128]{0:T(256)(128)(2,1)} %param.18) | copy-start | bytes 772
  306.0 12.3 %copy-start.11 = (u32[128]{0:T(128)S(1)}, u32[128]{0:T(128)}, u32[]{:S(2)}) copy-start(u32[128]{0:T(128)} %constant.65) | copy-start | bytes 1540
  306.0 152.8 %copy-start.8 = (f32[8,8]{1,0:T(8,128)S(1)}, f32[8,8]{1,0:T(8,128)}, u32[]{:S(2)}) copy-start(f32[8,8]{1,0:T(8,128)} %param.27) | copy-start | bytes 772
  306.0 154.7 %all-to-all-start.2 = ((bf16[128,4,7168]{2,1,0:T(4,128)(2,1)}), bf16[128,4,7168]{2,1,0:T(4,128)(2,1)}, u32[]{:S(2)}, u32[]{:S(2)}) async-start(bf16[128,4,7168]{2,1,0:T(4,128)(2,1)} %reshape.145), calls=%async_computation.2 | async-start | bytes 14680064 | tf_op jit(solution)/shard_map/all_to_all | solution.py:123
  460.7 19.4 %copy-start.1 = (bf16[16,512,128]{2,1,0:T(8,128)(2,1)S(1)}, bf16[16,512,128]{2,1,0:T(8,128)(2,1)}, u32[]{:S(2)}) copy-start(bf16[16,512,128]{2,1,0:T(8,128)(2,1)} %param.22) | copy-start | bytes 6291460
Sparse Core Ops, SparseCore 0:
  50.6 50.0 all-gather.4
  106.9 18.2 reduce-scatter.3
  128.3 136.1 all-gather.6
where the time goes:
time: 490 us; the launch traced here: 487 us
  blocking collectives  242 us (49%)
  local copies, waits for them, and re-layouts  78.4 us (16%)
  waiting for transfers between devices  66.2 us (14%)
  matrix products  43.5 us (9%)
  between operations  19.2 us (4%)
  starting transfers between devices  19.1 us (4%)
  other arithmetic  17.8 us (4%)
    unnamed x1, blocking collectives  137 us
    all_to_all x1, blocking collectives, body(): lax.all_to_all(copies, ('dp', 'tp'), split_axis=0, concat_axis=0, tiled=T...  105 us
    all_gather x1, waiting for transfers between devices, body(): lax.all_gather(head_out, 'dp', axis=0, tiled=True)  50.2 us
    unnamed x32, local copies, waits for them, and re-layouts  19.5 us
    dot_general x1, matrix products, body(): jnp.dot(hidden, w_down[0], preferred_element_type=jnp.float32)  16 us
    reshape x1, local copies, waits for them, and re-layouts, body(): returned = lax.all_to_all(jnp.dot(hidden, w_down[0], preferred_element_ty...  12.6 us
    reshape x1, local copies, waits for them, and re-layouts, body(): flat = rows.reshape(-1, width)  12.1 us
    gather x1, local copies, waits for them, and re-layouts, attend(): cache_pool[block_table].reshape(requests, context, cache_pool.shape[2])  11.8 us
  transfers between devices with their start and end apart: 5, of which 3 were waited for; matrix products, arithmetic and copies ran while one was open for 15% of the time, Pallas kernels for 0%

commit v1 on v0

--- a/solution.py
+++ b/solution.py
@@ -1,10 +1,360 @@
+import functools
 import jax
 import jax.numpy as jnp
 from jax import lax
+from jax.experimental import pallas as pl
+from jax.experimental.pallas import tpu as pltpu
 from jax.sharding import PartitionSpec as P
 
 softmax_scale = 192.0 ** (-0.5)
+MESH = pl.DeviceIdType.MESH
 norm_eps = 1e-06
+WIDE = 7168
+HALF = 3584
+PARTS = ((0, 1280), (1280, 1280), (2560, 1024))
+ORDER = ((0, 1, 2), (1, 2, 0), (2, 0, 1))
+TILE = 256
+
+
+class Links:
+    def __init__(self, send, recv):
+        self.send, self.recv, self.used = send, recv, 0
+        rank = lax.axis_index("dp")
+        self.core = lax.rem(rank, 2)
+        self.pos = (lax.axis_index("tp"), rank // 8, lax.rem(rank // 2, 4))
+
+    def device(self, pos, core):
+        return ((pos[1] * 4 + pos[2]) * 2 + core, pos[0])
+
+    def along(self, axis, step):
+        return lax.rem(self.pos[axis] + step, 4)
+
+    def near(self, axis, step):
+        pos = list(self.pos)
+        pos[axis] = self.along(axis, step)
+        return self.device(pos, self.core)
+
+    def twin(self):
+        return self.device(self.pos, 1 - self.core)
+
+    def copy(self, src, dst, device):
+        slot = self.used
+        self.used += 1
+        made = pltpu.make_async_remote_copy(
+            src_ref=src,
+            dst_ref=dst,
+            send_sem=self.send.at[slot],
+            recv_sem=self.recv.at[slot],
+            device_id=device,
+            device_id_type=MESH,
+        )
+        made.start()
+        return made
+
+
+def place(part, a, b, c):
+    index = [None, None, None]
+    for axis, value in zip(ORDER[part], (a, b, c)):
+        index[axis] = value
+    return tuple(index)
+
+
+ALL = slice(None)
+
+
+def expert_kernel(
+    s16, gain, coef, wg_in, wu_in, wd_in, out,
+    x0, x1, x2, t0, t1, t2, wg, wu, wd, accg, accu, hid,
+    r0, r1, r2, ca0, ca1, ca2, cb0, cb1, cb2, bb0, bb1, bb2, aa0, aa1, aa2,
+    sums, fin, load, send, recv,
+):
+    net = Links(send, recv)
+    core = net.core
+    x, t, r = (x0, x1, x2), (t0, t1, t2), (r0, r1, r2)
+    ca, cb, bb, aa = (ca0, ca1, ca2), (cb0, cb1, cb2), (bb0, bb1, bb2), (aa0, aa1, aa2)
+
+    barrier = pltpu.get_barrier_semaphore()
+    partners = [net.near(axis, k) for axis in range(3) for k in (1, 3, 2)] + [net.twin()]
+    for device in partners:
+        pl.semaphore_signal(barrier, inc=1, device_id=device, device_id_type=MESH)
+
+    loads = []
+    for half in range(2):
+        which = core if half == 0 else 1 - core
+        rows = pl.ds(pl.multiple_of(which * HALF, HALF), HALF)
+        for n, (src, dst) in enumerate(
+            ((wg_in.at[0, rows, :], wg.at[half]), (wu_in.at[0, rows, :], wu.at[half]), (wd_in.at[0, :, rows], wd.at[half]))
+        ):
+            made = pltpu.make_async_copy(src, dst, load.at[half * 3 + n])
+            made.start()
+            loads.append(made)
+
+    stream = s16[...]
+    power = jnp.sum(stream * stream, axis=1, keepdims=True)
+    sums[0] = jnp.broadcast_to(power, (16, 128))
+    pl.semaphore_wait(barrier, len(partners))
+    pair = net.copy(sums.at[0], sums.at[1], net.twin())
+    accg[...] = jnp.zeros_like(accg)
+    accu[...] = jnp.zeros_like(accu)
+    pair.wait()
+    power = (sums[0][:, 0:1] + sums[1][:, 0:1]) * (1.0 / WIDE)
+    scale = lax.rsqrt(power + norm_eps)
+    px, py, pz = net.pos
+    sent = []
+
+    def go(src, dst, device):
+        made = net.copy(src, dst, device)
+        sent.append(made)
+        return made
+
+    pa, pb, pc = [], [], []
+    for p, (off, width) in enumerate(PARTS):
+        cols = slice(off, off + width)
+        x[p][px, py, pz] = (s16[:, cols] * scale * gain[core][:, cols]).astype(jnp.bfloat16)
+    ga = []
+    for p in range(3):
+        block = x[p].at[px, py, pz]
+        ga.append([go(block, block, net.near(ORDER[p][0], k)) for k in (1, 3, 2)])
+
+    JS = (0, 1, 3, 2)
+    SLOT = {1: 1, 3: 0, 2: 2}
+    gb = [None] * 3
+    gc = [[None] * 4 for _ in range(3)]
+    gf = [[None] * 4 for _ in range(3)]
+    twins = []
+
+    def line(p, ref, jb, jc):
+        return ref.at[place(p, ALL, net.along(ORDER[p][1], jb), net.along(ORDER[p][2], jc))]
+
+    def to_twin(p, jb, jc):
+        made = go(line(p, x[p], jb, jc), line(p, t[p], jb, jc), net.twin())
+        twins.append((p, jb, jc, made))
+
+    def spread(p, n):
+        src = line(p, x[p], JS[n], 0)
+        gc[p][n] = [go(src, src, net.near(ORDER[p][2], k)) for k in (1, 3)]
+        to_twin(p, JS[n], 0)
+
+    def multiply(p, ref, jc, half):
+        off, width = PARTS[p]
+        where = place(p, ALL, ALL, net.along(ORDER[p][2], jc))
+
+        def step(k, carry):
+            lanes = pl.ds(pl.multiple_of(k * TILE, TILE), TILE)
+            rows = pl.ds(pl.multiple_of(off + k * TILE, TILE), TILE)
+            left = ref[where + (ALL, lanes)].reshape(256, TILE)
+            accg[where] += jnp.dot(left, wg[half, rows, :], preferred_element_type=jnp.float32).reshape(4, 4, 16, 256)
+            accu[where] += jnp.dot(left, wu[half, rows, :], preferred_element_type=jnp.float32).reshape(4, 4, 16, 256)
+            return carry
+
+        lax.fori_loop(0, width // TILE, step, 0)
+
+    for p in range(3):
+        for made in ga[p]:
+            made.wait_recv()
+        src = line(p, x[p], 0, 0)
+        gb[p] = [go(src, src, net.near(ORDER[p][1], k)) for k in (1, 3, 2)]
+        spread(p, 0)
+    for made in loads:
+        made.wait()
+    for n in (1, 2, 3):
+        for p in range(3):
+            gb[p][SLOT[JS[n]]].wait_recv()
+            spread(p, n)
+    for n in range(4):
+        for p in range(3):
+            gc[p][n][0].wait_recv()
+            gc[p][n][1].wait_recv()
+            if n % 2 == 0:
+                src = line(p, x[p], JS[n], 3)
+                gf[p][n] = go(src, src, net.near(ORDER[p][2], 1))
+            else:
+                src = line(p, x[p], JS[n], 1)
+                gf[p][n] = go(src, src, net.near(ORDER[p][2], 3))
+            to_twin(p, JS[n], 3)
+            to_twin(p, JS[n], 1)
+            if n == 0:
+                multiply(p, x[p], 0, 0)
+            if n == 1:
+                for q, jb, jc, made in twins:
+                    if q == p and jc == 0:
+                        made.wait_recv()
+                multiply(p, t[p], 0, 1)
+    for p in range(3):
+        multiply(p, x[p], 1, 0)
+        multiply(p, x[p], 3, 0)
+        for jc in (1, 3):
+            for q, jb, kc, made in twins:
+                if q == p and kc == jc:
+                    made.wait_recv()
+            multiply(p, t[p], jc, 1)
+    for p in range(3):
+        for n in range(4):
+            gf[p][n].wait_recv()
+            to_twin(p, JS[n], 2)
+        multiply(p, x[p], 2, 0)
+    for p in range(3):
+        for q, jb, kc, made in twins:
+            if q == p and kc == 2:
+                made.wait_recv()
+        multiply(p, t[p], 2, 1)
+    for made in sent:
+        made.wait_send()
+    sent.clear()
+
+    def activate(k, carry):
+        g = accg[k].reshape(256, 256)
+        u = accu[k].reshape(256, 256)
+        c = coef[k].reshape(256, 128)[:, 0:1]
+        hid[k] = (g * jax.nn.sigmoid(g) * u * c).astype(jnp.bfloat16).reshape(4, 4, 16, 256)
+        return carry
+
+    lax.fori_loop(0, 4, activate, 0)
+
+    def down_twin(p, jc):
+        off, width = PARTS[p]
+        where = place(p, ALL, ALL, net.along(ORDER[p][2], jc))
+
+        def step(k, carry):
+            lanes = pl.ds(pl.multiple_of(k * TILE, TILE), TILE)
+            cols = pl.ds(pl.multiple_of(off + k * TILE, TILE), TILE)
+            got = jnp.dot(hid[where].reshape(256, 256), wd[1, :, cols], preferred_element_type=jnp.float32)
+            t[p][where + (ALL, lanes)] = got.astype(jnp.bfloat16).reshape(4, 4, 16, TILE)
+            return carry
+
+        lax.fori_loop(0, width // TILE, step, 0)
+        return go(t[p].at[where], r[p].at[where], net.twin())
+
+    def down_own(p, jc, made):
+        off, width = PARTS[p]
+        where = place(p, ALL, ALL, net.along(ORDER[p][2], jc))
+        made.wait_recv()
+
+        def step(k, carry):
+            lanes = pl.ds(pl.multiple_of(k * TILE, TILE), TILE)
+            cols = pl.ds(pl.multiple_of(off + k * TILE, TILE), TILE)
+            got = jnp.dot(hid[where].reshape(256, 256), wd[0, :, cols], preferred_element_type=jnp.float32)
+            got = got + r[p][where + (ALL, lanes)].reshape(256, TILE).astype(jnp.float32)
+            x[p][where + (ALL, lanes)] = got.astype(jnp.bfloat16).reshape(4, 4, 16, TILE)
+            return carry
+
+        lax.fori_loop(0, width // TILE, step, 0)
+
+    JB = (2, 1, 3, 0)
+    PLUS, MINUS = (0, 3), (1, 2)
+    steps = [(p, jc) for jc in (2, 1, 3, 0) for p in range(3)]
+    made_twin = {}
+    h1, h2 = {}, {}
+
+    def add_line(p, jb, jc, others):
+        b, c = net.along(ORDER[p][1], jb), net.along(ORDER[p][2], jc)
+
+        def step(k, carry):
+            where = place(p, k, b, c)
+            total = x[p][where].astype(jnp.float32)
+            for ref, index in others:
+                total = total + ref[index + (k,)].astype(jnp.float32)
+            x[p][where] = total.astype(jnp.bfloat16)
+            return carry
+
+        lax.fori_loop(0, 4, step, 0)
+
+    def send_c1(p):
+        h1[p] = []
+        for i, n in enumerate(PLUS):
+            h1[p].append(go(line(p, x[p], JB[n], 2), ca[p].at[0, i], net.near(ORDER[p][2], 1)))
+        for i, n in enumerate(MINUS):
+            h1[p].append(go(line(p, x[p], JB[n], 2), ca[p].at[1, i], net.near(ORDER[p][2], 3)))
+
+    def send_c2(p, jc):
+        way = 0 if jc == 1 else 1
+        mine = PLUS if jc == 1 else MINUS
+        for i in range(2):
+            h1[p][way * 2 + i].wait_recv()
+        for n in range(4):
+            if n in mine:
+                add_line(p, JB[n], jc, [(ca[p], (way, mine.index(n)))])
+            h2[p, way, n] = go(line(p, x[p], JB[n], jc), cb[p].at[way, n], net.near(ORDER[p][2], jc))
+
+    made_twin[steps[0]] = down_twin(*steps[0])
+    for i, (p, jc) in enumerate(steps):
+        if i + 1 < len(steps):
+            made_twin[steps[i + 1]] = down_twin(*steps[i + 1])
+        down_own(p, jc, made_twin[p, jc])
+        if jc == 2:
+            send_c1(p)
+        elif jc != 0:
+            send_c2(p, jc)
+    hb = [[None] * 4 for _ in range(3)]
+    for n in range(3):
+        for p in range(3):
+            for way in range(2):
+                h2[p, way, n].wait_recv()
+            add_line(p, JB[n], 0, [(cb[p], (0, n)), (cb[p], (1, n))])
+            hb[p][n] = go(line(p, x[p], JB[n], 0), bb[p].at[n], net.near(ORDER[p][1], JB[n]))
+    for p in range(3):
+        for way in range(2):
+            h2[p, way, 3].wait_recv()
+        for n in range(3):
+            hb[p][n].wait_recv()
+        add_line(p, 0, 0, [(cb[p], (0, 3)), (cb[p], (1, 3))] + [(bb[p], (n,)) for n in range(3)])
+    haa = []
+    for p in range(3):
+        _, mb, mc = (net.pos[axis] for axis in ORDER[p])
+        for n, k in enumerate((2, 1, 3)):
+            src = x[p].at[place(p, net.along(ORDER[p][0], k), mb, mc)]
+            haa.append(go(src, aa[p].at[n], net.near(ORDER[p][0], k)))
+    for p, (off, width) in enumerate(PARTS):
+        for n in range(3):
+            haa[p * 3 + n].wait_recv()
+        total = x[p][px, py, pz].astype(jnp.float32)
+        for n in range(3):
+            total = total + aa[p][n].astype(jnp.float32)
+        fin[0, :, off:off + width] = s16[:, off:off + width] + total
+    theirs = fin.at[0, pl.ds(pl.multiple_of((1 - core) * 8, 8), 8)]
+    last = net.copy(theirs, fin.at[1, pl.ds(0, 8)], net.twin())
+    mine = fin[0, pl.ds(pl.multiple_of(core * 8, 8), 8)]
+    out[:, pl.ds(pl.multiple_of(core * HALF, HALF), HALF)] = mine.astype(jnp.bfloat16)
+    last.wait_recv()
+    out[:, pl.ds(pl.multiple_of((1 - core) * HALF, HALF), HALF)] = fin[1, 0:8].astype(jnp.bfloat16)
+    last.wait_send()
+    for made in sent:
+        made.wait_send()
+
+
+def experts(s16, gain, coef, w_gate, w_up, w_down):
+    bf = jnp.bfloat16
+    slots = 180
+    vm = pl.BlockSpec(memory_space=pltpu.VMEM)
+    hbm = pl.BlockSpec(memory_space=pl.ANY)
+    grid = [pltpu.VMEM((4, 4, 4, 16, w), bf) for _, w in PARTS]
+    return pl.pallas_call(
+        expert_kernel,
+        out_shape=jax.ShapeDtypeStruct((8, WIDE), bf),
+        in_specs=[vm, vm, vm, hbm, hbm, hbm],
+        out_specs=vm,
+        scratch_shapes=grid + grid + [
+            pltpu.VMEM((2, HALF, 256), bf),
+            pltpu.VMEM((2, HALF, 256), bf),
+            pltpu.VMEM((2, 256, HALF), bf),
+            pltpu.VMEM((4, 4, 4, 16, 256), jnp.float32),
+            pltpu.VMEM((4, 4, 4, 16, 256), jnp.float32),
+            pltpu.VMEM((4, 4, 4, 16, 256), bf),
+        ] + grid
+        + [pltpu.VMEM((2, 2, 4, 16, w), bf) for _, w in PARTS]
+        + [pltpu.VMEM((2, 4, 4, 16, w), bf) for _, w in PARTS]
+        + [pltpu.VMEM((3, 4, 16, w), bf) for _, w in PARTS]
+        + [pltpu.VMEM((3, 16, w), bf) for _, w in PARTS]
+        + [
+            pltpu.VMEM((2, 16, 128), jnp.float32),
+            pltpu.VMEM((2, 16, HALF), jnp.float32),
+            pltpu.SemaphoreType.DMA((6,)),
+            pltpu.SemaphoreType.DMA((slots,)),
+            pltpu.SemaphoreType.DMA((slots,)),
+        ],
+        compiler_params=pltpu.CompilerParams(collective_id=2, has_side_effects=True, vmem_limit_bytes=62 * 2**20),
+        name="experts",
+    )(s16, gain.reshape(2, 1, HALF), coef, w_gate, w_up, w_down)
 
 
 def attend(query, cache_pool, block_scale, block_table, lengths, value_up):
@@ -50,10 +400,8 @@
     w_down,
 ):
     ranks = lax.axis_size("dp")
-    groups = lax.axis_size("tp")
     rank = lax.axis_index("dp")
     requests = block_table.shape[0]
-    width = residual.shape[1]
     leaving = migration[:, 1] == rank
     local_req = jnp.sum(jnp.where(leaving, migration[:, 0] - rank * requests, 0))
     is_source = jnp.any(leaving)
@@ -91,48 +439,18 @@
     landed = lax.all_to_all(summed, "dp", split_axis=0, concat_axis=2, tiled=True)
     proj = landed.reshape(landed.shape[1], landed.shape[2])
     stream = residual.astype(jnp.float32) + proj.astype(jnp.float32)
-    power = jnp.mean(stream * stream, axis=1, keepdims=True)
-    normed = (stream * lax.rsqrt(power + norm_eps) * norm_gain[None, :]).astype(jnp.bfloat16)
-    tokens = normed.shape[0]
-    topk = expert_ids.shape[1]
-    experts = expert_owner.shape[0]
-    capacity = min(tokens, max(2, 2 * tokens * topk // experts))
-    picks = expert_ids[:, :, None] == jnp.arange(experts)[None, None, :]
-    named = jnp.sum(picks, axis=1)
-    before = jnp.cumsum(named, axis=0) - named
-    slots = jnp.sum(jnp.where(picks, before[:, None, :], 0), axis=2)
-    owners = jnp.sum(jnp.where(picks, expert_owner[None, None, :], 0), axis=2)
-    target = owners * capacity + slots
-    lanes = jnp.arange(ranks * capacity)
-    hits = lanes[:, None, None] == target[None, :, :]
-    placing = jnp.any(hits, axis=2).astype(jnp.bfloat16)
-    combine = jnp.transpose(jnp.sum(jnp.where(hits, gate_weights[None, :, :], 0.0), axis=2))
-    outgoing = (
-        jnp.dot(placing, normed, preferred_element_type=jnp.float32)
-        .astype(jnp.bfloat16)
-        .reshape(ranks, capacity, width)
-    )
-    copies = jnp.broadcast_to(outgoing[:, None], (ranks, groups, capacity, width)).reshape(
-        ranks * groups, capacity, width
-    )
-    rows = lax.all_to_all(copies, ("dp", "tp"), split_axis=0, concat_axis=0, tiled=True)
-    flat = rows.reshape(-1, width)
-    gate = jnp.dot(flat, w_gate[0], preferred_element_type=jnp.float32)
-    upper = jnp.dot(flat, w_up[0], preferred_element_type=jnp.float32)
-    hidden = (jax.nn.silu(gate) * upper).astype(jnp.bfloat16)
-    returned = lax.all_to_all(
-        jnp.dot(hidden, w_down[0], preferred_element_type=jnp.float32)
-        .astype(jnp.bfloat16)
-        .reshape(rows.shape),
-        ("dp", "tp"),
-        split_axis=0,
-        concat_axis=0,
-        tiled=True,
-    )
-    results = jnp.sum(returned.reshape(ranks, groups, capacity, width).astype(jnp.float32), axis=1)
-    flat_results = results.reshape(ranks * capacity, width)
-    moe = jnp.dot(combine, flat_results, precision=lax.Precision.HIGHEST)
-    mixed = (stream + moe).astype(jnp.bfloat16)
+    groups = [[2 * i, 2 * i + 1] for i in range(16)]
+    s16 = lax.all_to_all(
+        stream.reshape(8, 2, HALF), "dp", split_axis=1, concat_axis=0, axis_index_groups=groups, tiled=True
+    ).reshape(16, HALF)
+    owners = expert_owner[expert_ids]
+    picks = owners[:, :, None] == jnp.arange(ranks)[None, None, :]
+    shares = jnp.sum(jnp.where(picks, gate_weights[:, :, None], 0.0), axis=1)
+    shares = lax.all_gather(shares, ("dp", "tp"), axis=0, tiled=True)
+    coef = lax.dynamic_index_in_dim(shares, rank, 1, keepdims=False)
+    coef = coef.reshape(4, 4, 2, 4, 8).transpose(3, 0, 1, 2, 4).reshape(4, 4, 4, 16, 1)
+    coef = jnp.broadcast_to(coef, (4, 4, 4, 16, 128))
+    mixed = experts(s16, norm_gain, coef, w_gate, w_up, w_down)
     return (mixed, arrived_blocks[None], arrived_scales[None])
 
 

time: 490 us -> 386 us (0.79)
  blocking collectives: 242 us -> 126 us
  Pallas kernels: 0 us -> 107 us
  local copies, waits for them, and re-layouts: 78.4 us -> 43.8 us
  matrix products: 43.5 us -> 16.9 us
  other arithmetic: 17.8 us -> 6.43 us
  starting transfers between devices: 19.1 us -> 7.9 us
  waiting for transfers between devices: 66.2 us -> 57.5 us
    pallas_call x0 -> x1, Pallas kernels: none -> 107 us  [experts(): pl.pallas_call(expert_kernel, out_shape=jax.ShapeDtypeStruct((8, WIDE), b...]
    all_to_all x1, blocking collectives: 105 us -> 4.67 us  [body(): lax.all_to_all(stream.reshape(8, 2, HALF), 'dp', split_axis=1, concat_axi...]
    unnamed x1, blocking collectives: 137 us -> 65.2 us
    all_gather x0 -> x1, blocking collectives: none -> 56.4 us  [body(): shares = lax.all_gather(shares, ('dp', 'tp'), axis=0, tiled=True)]
    reshape x3 -> x1, local copies, waits for them, and re-layouts: 30 us -> 0.12 us  [body(): coef.reshape(4, 4, 2, 4, 8).transpose(3, 0, 1, 2, 4).reshape(4, 4, 4, 16, 1)]
    dot_general x4 -> x0, matrix products: 27.4 us -> none  [the longest x1 16 us: body(): jnp.dot(hidden, w_down[0], preferred_element_type=jnp.float32)]
    reduce_sum x5 -> x1, other arithmetic: 10.4 us -> 0.1 us  [body(): shares = jnp.sum(jnp.where(picks, gate_weights[:, :, None], 0.0), axis=1)]
    all_to_all x1 -> x0, starting transfers between devices: 9.67 us -> none  [body(): lax.all_to_all(jnp.dot(hidden, w_down[0], preferred_element_type=jnp.floa...]
  transfers between devices with their start and end apart: 5 -> 4, of which waited for: 3 -> 2; matrix products, arithmetic and copies ran while one was open for 15% -> 4% of each run, Pallas kernels for 0% -> 28%
where the time goes in v1:
time: 386 us; the launch traced here: 385 us
  blocking collectives  126 us (33%)
  Pallas kernels  107 us (28%)
  waiting for transfers between devices  57.5 us (15%)
  local copies, waits for them, and re-layouts  43.8 us (11%)
  between operations  19.3 us (5%)
  matrix products  16.9 us (4%)
  starting transfers between devices  7.9 us (2%)
  other arithmetic  6.43 us (2%)
    pallas_call x1, Pallas kernels, experts(): pl.pallas_call(expert_kernel, out_shape=jax.ShapeDtypeStruct((8, WIDE), b...  107 us
    unnamed x1, blocking collectives  65.2 us
    all_gather x1, blocking collectives, body(): shares = lax.all_gather(shares, ('dp', 'tp'), axis=0, tiled=True)  56.4 us
    all_gather x1, waiting for transfers between devices, body(): lax.all_gather(head_out, 'dp', axis=0, tiled=True)  50.2 us
    unnamed x35, local copies, waits for them, and re-layouts  21.1 us
    gather x1, local copies, waits for them, and re-layouts, attend(): cache_pool[block_table].reshape(requests, context, cache_pool.shape[2])  11.7 us
    sub x1, matrix products, attend(): expo = jnp.exp(scores - top)  7.93 us
    all_to_all x1, starting transfers between devices, body(): lax.all_to_all(summed, 'dp', split_axis=0, concat_axis=2, tiled=True)  7.78 us
  transfers between devices with their start and end apart: 4, of which 2 were waited for; matrix products, arithmetic and copies ran while one was open for 4% of the time, Pallas kernels for 28%

profile of v1, /device:TPU:1, one launch (start us, length us, event | category | flops | bytes accessed | tf_op | source)
XLA Modules:
  0.0 385.2 jit_solution(1391801188485752244)
XLA Ops:
  7.2 0.0 copy-start
  7.2 0.0 copy-start.6
  7.2 0.0 all-gather.5.cloned.1.call-start
  7.2 14.9 %copy.47 = bf16[128,64,576]{2,1,0:T(8,128)(2,1)} copy(bf16[128,64,576]{0,2,1:T(8,128)(2,1)} %param.17) | data formatting | bytes 18874368 | tf_op args[1]
  22.1 0.1 copy.46
  22.2 0.1 reshape.126
  22.3 0.0 copy-start.1
  22.3 0.0 copy-start.11
  22.3 11.7 %gather_fusion = bf16[128,64,576]{2,1,0:T(8,128)(2,1)} fusion(bf16[128,64,576]{2,1,0:T(8,128)(2,1)} %copy.47, s32[1024]{0:T(1024)S(1)} %pad_clamp_fusion.2), kind=kCustom, calls=%fused_computation | custom fusion | bytes 18874880 | tf_op jit(solution)/shard_map/gather | solution.py:365
  34.0 1.2 gather_fusion.1
  35.3 0.1 reshape.173
  35.4 0.1 broadcast_in_dim.75
  35.5 0.1 mul.28
  35.6 0.6 broadcast_multiply_fusion
  36.2 0.1 iota_compare_fusion.1
  36.3 7.9 %fusion.17 = (f32[32,16]{1,0:T(8,128)}, f32[32,16,256]{2,1,0:T(8,128)S(1)}) fusion(bf16[32,256,576]{2,1,0:T(8,128)(2,1)} %bitcast.42, bf16[32,16,576]{2,1,0:T(8,128)(2,1)} %param.16, f32[32,256]{1,0:T(8,128)} %broadcast_multiply_fusion, pred[32,256]{1,0:T(8,128)(4,1)S(1)} %iota_compare_fusion.1), kind=kOutput, calls=%fused_computation.49 | convolution fusion | flops 151519488 | bytes 10594304 | tf_op jit(solution)/shard_map/sub | solution.py:372
  44.2 4.7 %fusion.3 = bf16[32,16,512]{2,1,0:T(8,128)(2,1)S(1)} fusion(bf16[32,256,576]{2,1,0:T(8,128)(2,1)} %bitcast.43, f32[32,16,256]{2,1,0:T(8,128)S(1)} %get-tuple-element.8, f32[32,256]{1,0:T(8,128)} %copy-done.4, f32[32,16]{1,0:T(8,128)} %get-tuple-element.7), kind=kOutput, calls=%fused_computation.8 | convolution fusion | flops 134873088 | bytes 9486336 | tf_op jit(solution)/shard_map/rhp,rpc->rhc/dot_general | solution.py:375
  48.9 0.0 copy-start.12
  49.0 0.7 fusion.10
  49.7 0.0 copy-start.5
  49.7 0.7 copy.64
  50.3 0.0 all-gather.5.cloned.1.call-update
  50.4 0.0 reduce-scatter.4.cloned.1.call-start
  50.4 50.2 %all-gather.5.cloned.1.call-done = bf16[1024,2048]{1,0:T(8,128)(2,1)} async-done(((bf16[32,2048]{1,0:T(8,128)(2,1)}), bf16[1024,2048]{1,0:T(8,128)(2,1)}) %all-gather.5.cloned.1.call-update) | async-done | bytes 4194320 | tf_op jit(solution)/shard_map/all_gather | solution.py:429
  100.6 3.6 convolution_convert_fusion
  104.2 0.2 copy.51
  104.4 0.3 copy.63
  104.7 1.7 reshape.179
  106.3 0.0 reduce-scatter.4.cloned.1.call-update
  106.4 0.0 all-gather.7.cloned.1.call-start
  106.4 0.6 fusion.14
  109.0 0.2 dynamic-slice_reduce_fusion.1
  109.2 4.6 %gather_fusion.3 = bf16[4,64,576]{2,1,0:T(8,128)(2,1)S(1)} fusion(bf16[128,64,576]{2,1,0:T(8,128)(2,1)} %copy.47, s32[1024]{0:T(1024)S(1)} %pad_clamp_fusion), kind=kCustom, calls=%fused_computation.3 | custom fusion | bytes 589840 | tf_op jit(solution)/shard_map/gather | solution.py:409
  113.8 0.7 compare_reduce_fusion.1
  114.5 1.4 broadcast_select_fusion
  115.9 0.0 all-gather.7.cloned.1.call-update
  117.8 0.6 gather_fusion.4
  118.5 0.6 dynamic-slice
  119.7 0.6 broadcast_select_fusion.1
  120.3 0.2 dynamic-update-slice
  120.6 0.1 reshape.165
  120.7 0.1 reshape.142
  120.8 0.8 gather_fusion.2
  121.6 0.1 reshape.141
  121.7 0.1 select_reduce_fusion
  121.8 56.4 %all_gather.13 = f32[1024,32]{1,0:T(8,128)S(1)} all-gather(f32[8,32]{1,0:T(8,128)S(1)} %select_reduce_fusion), channel_id=1, replica_groups=mesh['dp'=32,'tp'=4] {'dp','tp'}, dimensions={0}, use_global_device_ids=true | all-gather | bytes 132096 | tf_op jit(solution)/shard_map/all_gather | solution.py:449
  178.2 0.4 dynamic-slice_reduce_fusion
  178.6 0.1 reshape.121
  178.8 0.1 broadcast_in_dim.80
  179.5 65.2 %all-reduce.1 = bf16[32,4]{1,0:T(8,128)(2,1)S(1)} all-reduce(bf16[32,4]{1,0:T(8,128)(2,1)S(1)} %reshape.165), channel_id=3, replica_groups=mesh['dp'=32,'tp'=4] {'dp'}, use_global_device_ids=true, to_apply=%add | all-reduce | flops 128 | bytes 512
  244.8 0.0 reduce-scatter.4.cloned.1.call-done
  244.8 1.1 reshape.180
  245.9 0.7 copy.57
  246.6 7.8 %all-to-all-start = ((bf16[32,8,224]{2,1,0:T(8,128)(2,1)}), bf16[32,8,224]{2,1,0:T(8,128)(2,1)S(1)}, u32[]{:S(2)}, u32[]{:S(2)}) async-start(bf16[32,8,224]{2,1,0:T(8,128)(2,1)} %copy.57), calls=%async_computation | async-start | bytes 262144 | tf_op jit(solution)/shard_map/all_to_all | solution.py:439
  254.4 0.5 broadcast_select_fusion.2
  254.9 7.3 %all-to-all-done = bf16[32,8,224]{2,1,0:T(8,128)(2,1)S(1)} async-done(((bf16[32,8,224]{2,1,0:T(8,128)(2,1)}), bf16[32,8,224]{2,1,0:T(8,128)(2,1)S(1)}, u32[]{:S(2)}, u32[]{:S(2)}) %all-to-all-start) | async-done | bytes 114720 | tf_op jit(solution)/shard_map/all_to_all | solution.py:439
  262.2 0.1 copy.52
  262.3 0.2 reshape.122
  262.6 4.7 %all_to_all.24 = f32[8,2,3584]{2,0,1:T(8,128)} all-to-all(f32[8,2,3584]{2,0,1:T(8,128)S(1)} %bitcast.46), channel_id=1, replica_groups={{0,4},{8,12},{16,20},{24,28},{32,36},{40,44},{48,52},{56,60},{64,68},{7..., dimensions={1} | all-to-all | bytes 458752 | tf_op jit(solution)/shard_map/all_to_all | solution.py:443
  267.2 1.0 broadcast_in_dim.81.coef
  268.2 107.1 %experts.1 = bf16[8,7168]{1,0:T(8,128)(2,1)} custom-call(f32[16,3584]{1,0:T(8,128)} %bitcast.47, f32[2,1,3584]{2,1,0:T(1,128)} %bitcast.51, f32[4,4,4,16,128]{4,3,2,1,0:T(8,128)} %broadcast_in_dim.81.coef, bf16[1,7168,256]{2,1,0:T(8,128)(2,1)} %wg_in.1, bf16[1,7168,256]{2,1,0:T(8,128)(2,1)} %wu_in.1, bf16[1,256,7168]{2,1,0:T(8,128)(2,1)} %wd_in.1), custom_call_target="tpu_custom_call" | custom-call | tf_op jit(solution)/shard_map/experts/pallas_call | solution.py:331
  375.4 0.0 all-gather.7.cloned.1.call-done
  375.4 1.7 dynamic-slice_select_fusion
  377.1 1.6 copy.67
  (30 shorter events, 0.2 us)
Async XLA Ops:
  7.2 93.4 %copy-start = (bf16[2048,224]{0,1:T(8,128)(2,1)S(1)}, bf16[2048,224]{0,1:T(8,128)(2,1)}, u32[]{:S(2)}) copy-start(bf16[2048,224]{0,1:T(8,128)(2,1)} %param.23) | copy-start | bytes 2752516
  7.2 14.9 %copy-start.6 = (s32[32,4]{0,1:T(4,128)S(1)}, s32[32,4]{0,1:T(4,128)}, u32[]{:S(2)}) copy-start(s32[32,4]{0,1:T(4,128)} %param.19) | copy-start | bytes 1540
  7.2 93.4 %all-gather.5.cloned.1.call-start = ((), (), s32[]{:S(2)}) async-start(), calls=%async_computation.3 | async-start | bytes 4325376 | tf_op jit(solution)/shard_map/all_gather | solution.py:429
  22.3 11.7 %copy-start.1 = (bf16[128]{0:T(256)(128)(2,1)S(1)}, bf16[128]{0:T(256)(128)(2,1)}, u32[]{:S(2)}) copy-start(bf16[128]{0:T(256)(128)(2,1)} %param.18) | copy-start | bytes 772
  22.3 13.9 %copy-start.11 = (s32[32]{0:T(128)S(1)}, s32[32]{0:T(128)}, u32[]{:S(2)}) copy-start(s32[32]{0:T(128)} %param.20) | copy-start | bytes 388
  35.6 0.7 copy-start.4
  36.3 12.6 %copy-start.3 = (bf16[16,512,128]{2,1,0:T(8,128)(2,1)S(1)}, bf16[16,512,128]{2,1,0:T(8,128)(2,1)}, u32[]{:S(2)}) copy-start(bf16[16,512,128]{2,1,0:T(8,128)(2,1)} %param.22) | copy-start | bytes 6291460
  44.2 64.8 %copy-start.7 = (s32[32,4]{0,1:T(4,128)S(1)}, s32[32,4]{0,1:T(4,128)}, u32[]{:S(2)}) copy-start(s32[32,4]{0,1:T(4,128)} %param.19) | copy-start | bytes 1540
  44.2 76.5 %copy-start.9 = (s32[8,8]{1,0:T(8,128)S(1)}, s32[8,8]{1,0:T(8,128)}, u32[]{:S(2)}) copy-start(s32[8,8]{1,0:T(8,128)} %param.26) | copy-start | bytes 772
  44.2 76.6 %copy-start.2 = (s32[32]{0:T(128)S(1)}, s32[32]{0:T(128)}, u32[]{:S(2)}) copy-start(s32[32]{0:T(128)} %param.28) | copy-start | bytes 388
  48.9 57.5 %copy-start.10 = (s32[16,3]{0,1:T(4,128)S(1)}, s32[16,3]{0,1:T(4,128)}, u32[]{:S(2)}) copy-start(s32[16,3]{0,1:T(4,128)} %param.21) | copy-start | bytes 580
  48.9 69.5 %copy-start.12 = (u32[128]{0:T(128)S(1)}, u32[128]{0:T(128)}, u32[]{:S(2)}) copy-start(u32[128]{0:T(128)} %constant.58) | copy-start | bytes 1540
  49.0 72.7 %copy-start.8 = (f32[8,8]{1,0:T(8,128)S(1)}, f32[8,8]{1,0:T(8,128)}, u32[]{:S(2)}) copy-start(f32[8,8]{1,0:T(8,128)} %param.27) | copy-start | bytes 772
  49.7 212.9 %copy-start.5 = (bf16[8,7168]{1,0:T(8,128)(2,1)S(1)}, bf16[8,7168]{1,0:T(8,128)(2,1)}, u32[]{:S(2)}) copy-start(bf16[8,7168]{1,0:T(8,128)(2,1)} %param.24) | copy-start | bytes 344068
  50.4 194.4 %reduce-scatter.4.cloned.1.call-start = ((), (), s32[]{:S(2)}) async-start(), calls=%async_computation.5 | async-start | bytes 573440
  106.4 269.0 %all-gather.7.cloned.1.call-start = ((), (), s32[]{:S(2)}) async-start(), calls=%async_computation.4 | async-start | bytes 10813440 | tf_op jit(solution)/shard_map/all_gather | solution.py:418
  246.6 15.6 %all-to-all-start = ((bf16[32,8,224]{2,1,0:T(8,128)(2,1)}), bf16[32,8,224]{2,1,0:T(8,128)(2,1)S(1)}, u32[]{:S(2)}, u32[]{:S(2)}) async-start(bf16[32,8,224]{2,1,0:T(8,128)(2,1)} %copy.57), calls=%async_computation | async-start | bytes 262144 | tf_op jit(solution)/shard_map/all_to_all | solution.py:439
Sparse Core Ops, SparseCore 0:
  50.5 50.0 all-gather.4
  106.5 18.3 reduce-scatter.3
  128.0 61.2 all-gather.6

commit v2 on v1

--- a/solution.py
+++ b/solution.py
@@ -6,12 +6,12 @@
 from jax.experimental.pallas import tpu as pltpu
 from jax.sharding import PartitionSpec as P
 
-softmax_scale = 192.0 ** (-0.5)
 MESH = pl.DeviceIdType.MESH
 norm_eps = 1e-06
 WIDE = 7168
 HALF = 3584
 PARTS = ((0, 1280), (1280, 1280), (2560, 1024))
+GRIDS = (1280, 1280, 1152)
 ORDER = ((0, 1, 2), (1, 2, 0), (2, 0, 1))
 TILE = 256
 
@@ -63,10 +63,10 @@
 
 
 def expert_kernel(
-    s16, gain, coef, wg_in, wu_in, wd_in, out,
+    s16, gain, ids, gates, owner, wg_in, wu_in, wd_in, out,
     x0, x1, x2, t0, t1, t2, wg, wu, wd, accg, accu, hid,
     r0, r1, r2, ca0, ca1, ca2, cb0, cb1, cb2, bb0, bb1, bb2, aa0, aa1, aa2,
-    sums, fin, load, send, recv,
+    sums, both, fin, load, send, recv,
 ):
     net = Links(send, recv)
     core = net.core
@@ -91,15 +91,30 @@
 
     stream = s16[...]
     power = jnp.sum(stream * stream, axis=1, keepdims=True)
-    sums[0] = jnp.broadcast_to(power, (16, 128))
+    sums[0, 0:16] = jnp.broadcast_to(power, (16, 128))
+    lane = lax.broadcasted_iota(jnp.int32, (1, 128), 1)
+    held = jnp.full((1, 128), -1, jnp.int32)
+    for e in range(32):
+        at = owner[e]
+        held = jnp.where(jnp.logical_or(lane == at, lane == at + 32), e, held)
+    share = jnp.zeros((8, 128), jnp.float32)
+    for k in range(8):
+        share = share + jnp.where(ids[:, k:k + 1] == held, gates[:, k:k + 1], 0.0)
+    sums[0, 16:24] = share
+    both[pl.ds(pl.multiple_of(core * 8, 8), 8)] = share
     pl.semaphore_wait(barrier, len(partners))
     pair = net.copy(sums.at[0], sums.at[1], net.twin())
     accg[...] = jnp.zeros_like(accg)
     accu[...] = jnp.zeros_like(accu)
     pair.wait()
-    power = (sums[0][:, 0:1] + sums[1][:, 0:1]) * (1.0 / WIDE)
+    power = (sums[0, 0:16][:, 0:1] + sums[1, 0:16][:, 0:1]) * (1.0 / WIDE)
     scale = lax.rsqrt(power + norm_eps)
+    both[pl.ds(pl.multiple_of((1 - core) * 8, 8), 8)] = sums[1, 16:24]
+    share = both[...]
+    high = share.astype(jnp.bfloat16)
+    rest = (share - high.astype(jnp.float32)).astype(jnp.bfloat16)
     px, py, pz = net.pos
+    x[2][px, py, pz, :, 1024:1152] = jnp.where(lane < 32, high, rest)
     sent = []
 
     def go(src, dst, device):
@@ -107,10 +122,9 @@
         sent.append(made)
         return made
 
-    pa, pb, pc = [], [], []
     for p, (off, width) in enumerate(PARTS):
         cols = slice(off, off + width)
-        x[p][px, py, pz] = (s16[:, cols] * scale * gain[core][:, cols]).astype(jnp.bfloat16)
+        x[p][px, py, pz, :, 0:width] = (s16[:, cols] * scale * gain[core][:, cols]).astype(jnp.bfloat16)
     ga = []
     for p in range(3):
         block = x[p].at[px, py, pz]
@@ -202,10 +216,14 @@
         made.wait_send()
     sent.clear()
 
+    rank = lax.axis_index("dp")
+    mine = jnp.logical_or(lane == rank, lane == rank + 32)
+
     def activate(k, carry):
         g = accg[k].reshape(256, 256)
         u = accu[k].reshape(256, 256)
-        c = coef[k].reshape(256, 128)[:, 0:1]
+        c = x[2][k, :, :, :, 1024:1152].reshape(256, 128).astype(jnp.float32)
+        c = jnp.sum(jnp.where(mine, c, 0.0), axis=1, keepdims=True)
         hid[k] = (g * jax.nn.sigmoid(g) * u * c).astype(jnp.bfloat16).reshape(4, 4, 16, 256)
         return carry
 
@@ -223,7 +241,7 @@
             return carry
 
         lax.fori_loop(0, width // TILE, step, 0)
-        return go(t[p].at[where], r[p].at[where], net.twin())
+        return go(t[p].at[where + (ALL, pl.ds(0, width))], r[p].at[where], net.twin())
 
     def down_own(p, jc, made):
         off, width = PARTS[p]
@@ -250,7 +268,7 @@
         b, c = net.along(ORDER[p][1], jb), net.along(ORDER[p][2], jc)
 
         def step(k, carry):
-            where = place(p, k, b, c)
+            where = place(p, k, b, c) + (ALL, pl.ds(0, PARTS[p][1]))
             total = x[p][where].astype(jnp.float32)
             for ref, index in others:
                 total = total + ref[index + (k,)].astype(jnp.float32)
@@ -259,12 +277,16 @@
 
         lax.fori_loop(0, 4, step, 0)
 
+    def out_line(p, jb, jc):
+        where = place(p, ALL, net.along(ORDER[p][1], jb), net.along(ORDER[p][2], jc))
+        return x[p].at[where + (ALL, pl.ds(0, PARTS[p][1]))]
+
     def send_c1(p):
         h1[p] = []
         for i, n in enumerate(PLUS):
-            h1[p].append(go(line(p, x[p], JB[n], 2), ca[p].at[0, i], net.near(ORDER[p][2], 1)))
+            h1[p].append(go(out_line(p, JB[n], 2), ca[p].at[0, i], net.near(ORDER[p][2], 1)))
         for i, n in enumerate(MINUS):
-            h1[p].append(go(line(p, x[p], JB[n], 2), ca[p].at[1, i], net.near(ORDER[p][2], 3)))
+            h1[p].append(go(out_line(p, JB[n], 2), ca[p].at[1, i], net.near(ORDER[p][2], 3)))
 
     def send_c2(p, jc):
         way = 0 if jc == 1 else 1
@@ -274,7 +296,7 @@
         for n in range(4):
             if n in mine:
                 add_line(p, JB[n], jc, [(ca[p], (way, mine.index(n)))])
-            h2[p, way, n] = go(line(p, x[p], JB[n], jc), cb[p].at[way, n], net.near(ORDER[p][2], jc))
+            h2[p, way, n] = go(out_line(p, JB[n], jc), cb[p].at[way, n], net.near(ORDER[p][2], jc))
 
     made_twin[steps[0]] = down_twin(*steps[0])
     for i, (p, jc) in enumerate(steps):
@@ -291,7 +313,7 @@
             for way in range(2):
                 h2[p, way, n].wait_recv()
             add_line(p, JB[n], 0, [(cb[p], (0, n)), (cb[p], (1, n))])
-            hb[p][n] = go(line(p, x[p], JB[n], 0), bb[p].at[n], net.near(ORDER[p][1], JB[n]))
+            hb[p][n] = go(out_line(p, JB[n], 0), bb[p].at[n], net.near(ORDER[p][1], JB[n]))
     for p in range(3):
         for way in range(2):
             h2[p, way, 3].wait_recv()
@@ -302,12 +324,12 @@
     for p in range(3):
         _, mb, mc = (net.pos[axis] for axis in ORDER[p])
         for n, k in enumerate((2, 1, 3)):
-            src = x[p].at[place(p, net.along(ORDER[p][0], k), mb, mc)]
+            src = x[p].at[place(p, net.along(ORDER[p][0], k), mb, mc) + (ALL, pl.ds(0, PARTS[p][1]))]
             haa.append(go(src, aa[p].at[n], net.near(ORDER[p][0], k)))
     for p, (off, width) in enumerate(PARTS):
         for n in range(3):
             haa[p * 3 + n].wait_recv()
-        total = x[p][px, py, pz].astype(jnp.float32)
+        total = x[p][px, py, pz, :, 0:width].astype(jnp.float32)
         for n in range(3):
             total = total + aa[p][n].astype(jnp.float32)
         fin[0, :, off:off + width] = s16[:, off:off + width] + total
@@ -322,16 +344,16 @@
         made.wait_send()
 
 
-def experts(s16, gain, coef, w_gate, w_up, w_down):
+def experts(s16, gain, ids, gates, owner, w_gate, w_up, w_down):
     bf = jnp.bfloat16
     slots = 180
     vm = pl.BlockSpec(memory_space=pltpu.VMEM)
     hbm = pl.BlockSpec(memory_space=pl.ANY)
-    grid = [pltpu.VMEM((4, 4, 4, 16, w), bf) for _, w in PARTS]
+    grid = [pltpu.VMEM((4, 4, 4, 16, w), bf) for w in GRIDS]
     return pl.pallas_call(
         expert_kernel,
         out_shape=jax.ShapeDtypeStruct((8, WIDE), bf),
-        in_specs=[vm, vm, vm, hbm, hbm, hbm],
+        in_specs=[vm, vm, vm, vm, pl.BlockSpec(memory_space=pltpu.SMEM), hbm, hbm, hbm],
         out_specs=vm,
         scratch_shapes=grid + grid + [
             pltpu.VMEM((2, HALF, 256), bf),
@@ -340,13 +362,14 @@
             pltpu.VMEM((4, 4, 4, 16, 256), jnp.float32),
             pltpu.VMEM((4, 4, 4, 16, 256), jnp.float32),
             pltpu.VMEM((4, 4, 4, 16, 256), bf),
-        ] + grid
+        ] + [pltpu.VMEM((4, 4, 4, 16, w), bf) for _, w in PARTS]
         + [pltpu.VMEM((2, 2, 4, 16, w), bf) for _, w in PARTS]
         + [pltpu.VMEM((2, 4, 4, 16, w), bf) for _, w in PARTS]
         + [pltpu.VMEM((3, 4, 16, w), bf) for _, w in PARTS]
         + [pltpu.VMEM((3, 16, w), bf) for _, w in PARTS]
         + [
-            pltpu.VMEM((2, 16, 128), jnp.float32),
+            pltpu.VMEM((2, 24, 128), jnp.float32),
+            pltpu.VMEM((16, 128), jnp.float32),
             pltpu.VMEM((2, 16, HALF), jnp.float32),
             pltpu.SemaphoreType.DMA((6,)),
             pltpu.SemaphoreType.DMA((slots,)),
@@ -354,104 +377,362 @@
         ],
         compiler_params=pltpu.CompilerParams(collective_id=2, has_side_effects=True, vmem_limit_bytes=62 * 2**20),
         name="experts",
-    )(s16, gain.reshape(2, 1, HALF), coef, w_gate, w_up, w_down)
-
-
-def attend(query, cache_pool, block_scale, block_table, lengths, value_up):
-    requests = block_table.shape[0]
-    block_size = cache_pool.shape[1]
-    latent = value_up.shape[1]
-    context = block_table.shape[1] * block_size
-    tiles = cache_pool[block_table].reshape(requests, context, cache_pool.shape[2])
-    pos_scale = jnp.repeat(block_scale[block_table].astype(jnp.float32), block_size, axis=1)
-    scores = jnp.einsum("rhc,rpc->rhp", query, tiles, preferred_element_type=jnp.float32)
-    scores = scores * softmax_scale * pos_scale[:, None, :]
-    live = jnp.arange(context)[None, :] < lengths[:, None]
-    scores = jnp.where(live[:, None, :], scores, -1e30)
-    top = jnp.max(scores, axis=2, keepdims=True)
-    expo = jnp.exp(scores - top)
-    weight = expo / jnp.sum(expo, axis=2, keepdims=True)
-    coef = (weight * pos_scale[:, None, :]).astype(jnp.bfloat16)
-    latent_out = jnp.einsum(
-        "rhp,rpc->rhc", coef, tiles[:, :, :latent], preferred_element_type=jnp.float32
-    ).astype(jnp.bfloat16)
-    head_out = jnp.einsum(
-        "rhc,hcv->rhv", latent_out, value_up, preferred_element_type=jnp.float32
-    ).astype(jnp.bfloat16)
-    return head_out.reshape(requests, -1)
+    )(s16, gain.reshape(2, 1, HALF), ids, gates, owner, w_gate, w_up, w_down)
+
+
+softmax_scale = 192.0 ** (-0.5)
+OWN = 224
+WITHIN = (((0,), (0,)), ((), ()))
+LAST = (((1,), (1,)), ((), ()))
+MIG = ((0, 32, 1, 2), (32, 48, 2, 1))
+
+
+def attend_kernel(
+    query, pool, table, scales, lens_s, mig_s, value_up, out_w, residual,
+    s16, blocks_out, scales_out,
+    kt, kp, hot, vu, wt, lat, h00, h01, h10, h11, n00, n01, n10, n11, part, px, rx, sp, gx, res, mg, quarter, lane_scale, row,
+    load, send, recv, recv2, send2,
+):
+    net = Links(send, recv)
+    core = net.core
+    x, y, z = net.pos
+    rank = (y * 4 + z) * 2 + core
+    heads = ((h00, h01), (h10, h11))
+    twin_heads = ((n00, n01), (n10, n11))
+    f32, bf = jnp.float32, jnp.bfloat16
+
+    loads = []
+    for i in range(8):
+        made = pltpu.make_async_copy(pool.at[pl.ds(i * 8, 8)], kt.at[pl.ds(i * 8, 8)], load.at[i])
+        made.start()
+        loads.append(made)
+    late = []
+    for i, (src, dst) in enumerate(((value_up, vu), (out_w, wt.at[pl.ds(0, OWN)]))):
+        made = pltpu.make_async_copy(src, dst, load.at[8 + i])
+        made.start()
+        late.append(made)
+
+    barrier = pltpu.get_barrier_semaphore()
+    for k in range(1, 32):
+        other = lax.rem(rank + k, 32)
+        pl.semaphore_signal(barrier, inc=1, device_id=(other, x), device_id_type=MESH)
+    for k in range(1, 4):
+        pl.semaphore_signal(barrier, inc=1, device_id=net.near(0, k), device_id_type=MESH)
+
+    rows = lax.broadcasted_iota(jnp.int32, (32, 128), 0)
+    widen = (rows == lax.broadcasted_iota(jnp.int32, (32, 128), 1) // 4).astype(f32)
+    names = jnp.dot(table[...].astype(f32), widen, preferred_element_type=f32)
+    held = lax.broadcasted_iota(jnp.int32, (4, 128), 0) == lax.rem(lax.broadcasted_iota(jnp.int32, (4, 128), 1), 4)
+    names = jnp.sum(jnp.where(held, names, 0.0), axis=0, keepdims=True)
+    names = jnp.broadcast_to(names, (128, 128))
+    turned = (names == lax.broadcasted_iota(jnp.int32, (128, 128), 0).astype(f32)).astype(f32)
+    hot[0:128] = turned.T.astype(bf)
+    leaving, sender, has_in = 0, 0, 0
+    for i in range(16):
+        goes = mig_s[1, i] == rank
+        leaving += jnp.where(goes, mig_s[0, i] - rank * 32, 0)
+        comes = mig_s[2, i] == rank
+        sender += jnp.where(comes, mig_s[1, i], 0)
+        has_in += jnp.where(comes, 1, 0)
+    slot = leaving * 4 + x
+    only = lax.broadcasted_iota(jnp.int32, (128, 128), 0) == slot
+    only = jnp.sum(jnp.where(only, hot[0:128].astype(f32), 0.0), axis=0, keepdims=True)
+    hot[128:144] = jnp.broadcast_to(only, (16, 128)).astype(bf)
+    slot_scale = jnp.dot(jnp.broadcast_to(scales[...].astype(f32), (16, 128)).astype(bf), turned.astype(bf), preferred_element_type=f32)[0:8]
+    groups = lax.broadcasted_iota(jnp.int32, (8, 128), 0) == lax.broadcasted_iota(jnp.int32, (8, 128), 1) // 16
+    spread = (
+        lax.rem(lax.broadcasted_iota(jnp.int32, (128, 1024), 0), 16)
+        == lax.rem(lax.broadcasted_iota(jnp.int32, (128, 1024), 1), 16)
+    ).astype(bf)
+    lane_scale[...] = jnp.dot(jnp.where(groups, slot_scale, 0.0).astype(bf), spread, preferred_element_type=f32).reshape(8, 1, 1024)
+    wt[pl.ds(OWN, 32)] = jnp.zeros((32, 2048), bf)
+
+    for i in range(8):
+        loads[i].wait()
+
+        def turn(k, carry):
+            for n in range(2):
+                at = i * 8 + k * 2 + n
+                got = lax.dot_general(hot[...], kt[at], LAST, preferred_element_type=f32)
+                kp[at] = got[0:128].astype(bf)
+                row[pl.ds(at, 1)] = got[128:129]
+            return carry
+
+        lax.fori_loop(0, 4, turn, 0)
+
+    its = jnp.sum(jnp.where(lax.broadcasted_iota(jnp.int32, (8, 128), 1) == slot, slot_scale, 0.0)[0:1], axis=1, keepdims=True)
+    mg[core, y, z, 0:64] = row[...].astype(bf)
+    mg[core, y, z, 64:80] = jnp.broadcast_to(its, (16, 576)).astype(bf)
+
+    pl.semaphore_wait(barrier, 34)
+    sent = []
+
+    def go(src, dst, device):
+        made = net.copy(src, dst, device)
+        sent.append(made)
+        return made
+
+    mine = residual[:, pl.ds(pl.multiple_of(core * HALF, HALF), HALF)].astype(f32)
+    rows = pl.ds(pl.multiple_of(core * 8, 8), 8)
+    res[0, rows] = mine
+    res[1, rows] = residual[:, pl.ds(pl.multiple_of((1 - core) * HALF, HALF), HALF)].astype(f32)
+    swap = go(res.at[1, rows], res.at[0, rows], net.twin())
+
+    def mig_line(i, first):
+        off, n, a, b = MIG[i]
+        r = pl.ds(off, n)
+        return mg.at[core, first, :, r] if a == 2 else mg.at[core, :, first, r]
+
+    m1 = []
+    for off, n, a, b in MIG:
+        src = mg.at[core, y, z, pl.ds(off, n)]
+        m1.append([go(src, src, net.near(a, k)) for k in (1, 3, 2)])
+    m2, mt = [None, None], []
+
+    def mig_spread(i):
+        off, n, a, b = MIG[i]
+        for made in m1[i]:
+            made.wait_recv()
+        src = mig_line(i, net.pos[b])
+        m2[i] = [go(src, src, net.near(b, k)) for k in (1, 3, 2)]
+        mt.append(go(src, src, net.twin()))
+
+    def mig_twin(i):
+        b = MIG[i][3]
+        for k, made in zip((1, 3, 2), m2[i]):
+            made.wait_recv()
+            src = mig_line(i, net.along(b, 4 - k))
+            mt.append(go(src, src, net.twin()))
+
+    def attend(g, carry):
+        q = query[pl.ds(g * 4, 4)].reshape(64, 576)
+        keys = kp[:, pl.ds(pl.multiple_of(g * 16, 16), 16), :].reshape(1024, 576)
+        scale = lane_scale[g]
+        score = lax.dot_general(q, keys, LAST, preferred_element_type=f32)
+        lane = lax.broadcasted_iota(jnp.int32, (1, 1024), 1)
+        which = lax.rem(lane, 16)
+        owner = which // 4
+        place_ = lax.rem(which, 4) * 64 + lane // 16
+        limit = jnp.where(owner == 0, lens_s[g * 4], jnp.where(owner == 1, lens_s[g * 4 + 1], jnp.where(owner == 2, lens_s[g * 4 + 2], lens_s[g * 4 + 3])))
+        holder = jnp.where(place_ < limit, owner, -1)
+        live = holder == lax.broadcasted_iota(jnp.int32, (64, 1024), 0) // 16
+        score = jnp.where(live, score * (scale * softmax_scale), -1e30)
+        top = jnp.max(score, axis=1, keepdims=True)
+        expo = jnp.exp(score - top)
+        total = jnp.sum(expo, axis=1, keepdims=True)
+        coef = (expo * (1.0 / total) * scale).astype(bf)
+        got = jnp.dot(coef, keys[:, 0:512], preferred_element_type=f32)
+        for n in range(4):
+            lat[n, pl.ds(pl.multiple_of(g * 64, 64), 64)] = got[:, n * 128:(n + 1) * 128]
+        return carry
+
+    ga = [[None] * 2, [None] * 2]
+    gb = [[None] * 2, [None] * 2]
+    tw = [[[], []], [[], []]]
+    AXES = ((1, 2), (2, 1))
+
+    def value_map(half):
+        for h in range(16):
+            rows = [lat[n, pl.ds(half * 256 + h, 16, stride=16), :] for n in range(4)]
+            rows = jnp.concatenate(rows, axis=1).astype(bf)
+            got = jnp.dot(rows, vu[h], preferred_element_type=f32).astype(bf)
+            heads[half][h // 8][y, z, :, (h % 8) * 128:(h % 8 + 1) * 128] = got
+
+    def head_line(ref, p, first):
+        return ref.at[first] if p == 0 and False else (ref.at[:, first] if AXES[p][0] == 1 else ref.at[first])
+
+    def head_start(half):
+        for p in range(2):
+            src = heads[half][p].at[y, z]
+            ga[half][p] = [go(src, src, net.near(AXES[p][0], k)) for k in (1, 3, 2)]
+
+    def head_twin(half, p, first):
+        tw[half][p].append(go(head_line(heads[half][p], p, first), head_line(twin_heads[half][p], p, first), net.twin()))
+
+    def head_spread(half):
+        for p in range(2):
+            for made in ga[half][p]:
+                made.wait_recv()
+            first = net.pos[AXES[p][1]]
+            src = head_line(heads[half][p], p, first)
+            gb[half][p] = [go(src, src, net.near(AXES[p][1], k)) for k in (1, 3, 2)]
+            head_twin(half, p, first)
+
+    def head_finish(half):
+        for i in range(3):
+            for p in range(2):
+                gb[half][p][i].wait_recv()
+                head_twin(half, p, net.along(AXES[p][1], 4 - (1, 3, 2)[i]))
+
+    def project(half, refs, who):
+        def step(k, carry):
+            total = lax.dot_general(refs[0][k].reshape(64, 1024), wt[:, 0:1024], LAST, preferred_element_type=f32)
+            total += lax.dot_general(refs[1][k].reshape(64, 1024), wt[:, 1024:2048], LAST, preferred_element_type=f32)
+            part[half, who, k] = total.reshape(4, 16, 256)
+            return carry
+
+        lax.fori_loop(0, 4, step, 0)
+
+    lax.fori_loop(0, 2, attend, 0)
+    mig_spread(0)
+    mig_spread(1)
+    lax.fori_loop(2, 4, attend, 0)
+    for made in late:
+        made.wait()
+    value_map(0)
+    head_start(0)
+    lax.fori_loop(4, 6, attend, 0)
+    head_spread(0)
+    lax.fori_loop(6, 8, attend, 0)
+    value_map(1)
+    head_start(1)
+    mig_twin(0)
+    mig_twin(1)
+    for made in mt:
+        made.wait_recv()
+    found = mg[lax.rem(sender, 2), sender // 8, lax.rem(sender // 2, 4)]
+    quarter[x] = jnp.where(has_in > 0, found, jnp.zeros_like(found))
+    mx = [go(quarter.at[x], quarter.at[x], net.near(0, k)) for k in (1, 3, 2)]
+    head_spread(1)
+    head_finish(0)
+    project(0, heads[0], core)
+    for p in range(2):
+        for made in tw[0][p]:
+            made.wait_recv()
+    project(0, twin_heads[0], 1 - core)
+
+    def shares(half):
+        for n in range(2):
+            rows = pl.ds(n * 8, 8)
+            both = jnp.concatenate([part[half, 0, :, :, rows], part[half, 1, :, :, rows]], axis=2)
+            px[half * 2 + n] = both.astype(bf)
+
+    shares(0)
+    head_finish(1)
+    project(1, heads[1], core)
+    for p in range(2):
+        for made in tw[1][p]:
+            made.wait_recv()
+    project(1, twin_heads[1], 1 - core)
+    shares(1)
+    back = [go(px.at[net.along(0, k)], rx.at[n], net.near(0, k)) for n, k in enumerate((1, 3, 2))]
+    for made in mx:
+        made.wait_recv()
+    for i in range(4):
+        blocks_out[i] = quarter[i, 0:64]
+        scales_out[i] = quarter[i, 64:80, 0:128]
+    for made in back:
+        made.wait_recv()
+
+    def add(k, carry):
+        total = px[x, k].astype(f32)
+        for n in range(3):
+            total = total + rx[n, k].astype(f32)
+        sp[k] = total.astype(bf)
+        return carry
+
+    lax.fori_loop(0, 4, add, 0)
+    to_core = y // 2
+    here = (lax.rem(y, 2) * 4 + z) * 2 + core
+    away = []
+    for k in range(16):
+        ty, tz = net.along(1, k // 4), net.along(2, k % 4)
+        made = pltpu.make_async_remote_copy(
+            src_ref=sp.at[ty, tz], dst_ref=gx.at[here], send_sem=send2.at[k], recv_sem=recv2.at[here],
+            device_id=net.device((x, ty, tz), to_core), device_id_type=MESH,
+        )
+        away.append(made)
+        if k:
+            made.start()
+
+    @pl.when(to_core != core)
+    def _():
+        away[0].start()
+
+    @pl.when(to_core == core)
+    def _():
+        gx[here] = sp[y, z]
+
+    swap.wait_recv()
+    for j in range(16):
+        made = pltpu.make_async_remote_copy(
+            src_ref=sp.at[0, 0], dst_ref=gx.at[j], send_sem=send2.at[j], recv_sem=recv2.at[j],
+            device_id=net.twin(), device_id_type=MESH,
+        )
+
+        @pl.when(jnp.logical_or(to_core != core, here != j))
+        def _():
+            made.wait_recv()
+
+        cols = slice(j * OWN, (j + 1) * OWN)
+        s16[:, cols] = res[0, :, cols] + gx[j].astype(f32)[:, 0:OWN]
+    for k in range(1, 16):
+        away[k].wait_send()
+
+    @pl.when(to_core != core)
+    def _():
+        away[0].wait_send()
+
+    for made in sent:
+        made.wait_send()
+
+
+def attend_all(query, pool, block_scale, table, lengths, migration, value_up, out_weight, residual):
+    bf, f32 = jnp.bfloat16, jnp.float32
+    vm = pl.BlockSpec(memory_space=pltpu.VMEM)
+    sm = pl.BlockSpec(memory_space=pltpu.SMEM)
+    hbm = pl.BlockSpec(memory_space=pl.ANY)
+    head = [pltpu.VMEM((4, 4, 16, 1024), bf)] * 8
+    return pl.pallas_call(
+        attend_kernel,
+        out_shape=(
+            jax.ShapeDtypeStruct((16, HALF), f32),
+            jax.ShapeDtypeStruct((4, 64, 576), bf),
+            jax.ShapeDtypeStruct((4, 16, 128), bf),
+        ),
+        in_specs=[vm, hbm, vm, vm, sm, sm, hbm, hbm, vm],
+        out_specs=(vm, vm, vm),
+        scratch_shapes=[
+            pltpu.VMEM((64, 576, 128), bf),
+            pltpu.VMEM((64, 128, 576), bf),
+            pltpu.VMEM((144, 128), bf),
+            pltpu.VMEM((16, 512, 128), bf),
+            pltpu.VMEM((256, 2048), bf),
+            pltpu.VMEM((4, 512, 128), f32),
+        ] + head + [
+            pltpu.VMEM((2, 2, 4, 4, 16, 256), f32),
+            pltpu.VMEM((4, 4, 4, 16, 256), bf),
+            pltpu.VMEM((3, 4, 4, 16, 256), bf),
+            pltpu.VMEM((4, 4, 16, 256), bf),
+            pltpu.VMEM((16, 16, 256), bf),
+            pltpu.VMEM((2, 16, HALF), f32),
+            pltpu.VMEM((2, 4, 4, 80, 576), bf),
+            pltpu.VMEM((4, 80, 576), bf),
+            pltpu.VMEM((8, 1, 1024), f32),
+            pltpu.VMEM((64, 576), f32),
+            pltpu.SemaphoreType.DMA((10,)),
+            pltpu.SemaphoreType.DMA((90,)),
+            pltpu.SemaphoreType.DMA((90,)),
+            pltpu.SemaphoreType.DMA((16,)),
+            pltpu.SemaphoreType.DMA((16,)),
+        ],
+        compiler_params=pltpu.CompilerParams(collective_id=1, has_side_effects=True, vmem_limit_bytes=62 * 2**20),
+        name="attend",
+    )(
+        query, jnp.transpose(pool, (1, 2, 0)), table.T, block_scale.reshape(1, 128), lengths,
+        migration.T, value_up, out_weight.T, residual,
+    )
 
 
 def body(
-    query,
-    cache_pool,
-    block_scale,
-    block_table,
-    lengths,
-    migration,
-    value_up,
-    out_weight,
-    residual,
-    norm_gain,
-    expert_ids,
-    gate_weights,
-    expert_owner,
-    w_gate,
-    w_up,
-    w_down,
+    query, cache_pool, block_scale, block_table, lengths, migration, value_up, out_weight, residual, norm_gain,
+    expert_ids, gate_weights, expert_owner, w_gate, w_up, w_down,
 ):
-    ranks = lax.axis_size("dp")
-    rank = lax.axis_index("dp")
-    requests = block_table.shape[0]
-    leaving = migration[:, 1] == rank
-    local_req = jnp.sum(jnp.where(leaving, migration[:, 0] - rank * requests, 0))
-    is_source = jnp.any(leaving)
-    out_rows = lax.dynamic_index_in_dim(block_table, local_req, 0, keepdims=False)
-    out_blocks = jnp.where(is_source, cache_pool[out_rows], 0)[None]
-    out_scales = jnp.where(is_source, block_scale[out_rows], 0)[None]
-    coming = migration[:, 2] == rank
-    sender = jnp.sum(jnp.where(coming, migration[:, 1], 0))
-    has_in = jnp.any(coming)
-    empty = (
-        jnp.zeros(out_blocks.shape[1:], jnp.bfloat16),
-        jnp.zeros(out_scales.shape[1:], jnp.bfloat16),
+    s16, blocks, scales = attend_all(
+        query, cache_pool, block_scale, block_table, lengths, migration, value_up, out_weight, residual
     )
-    blocks = lax.all_gather(out_blocks, "dp", axis=0, tiled=True)
-    scales = lax.all_gather(out_scales, "dp", axis=0, tiled=True)
-    inside = has_in & (sender >= 0) & (sender < blocks.shape[0])
-    chosen = jnp.clip(sender, 0, blocks.shape[0] - 1)
-    pick_blocks = lax.dynamic_index_in_dim(blocks, chosen, 0, keepdims=False)
-    pick_scales = lax.dynamic_index_in_dim(scales, chosen, 0, keepdims=False)
-    arrived_blocks = jnp.where(inside, pick_blocks, empty[0])
-    arrived_scales = jnp.where(inside, pick_scales, empty[1])
-    head_out = attend(query, cache_pool, block_scale, block_table, lengths, value_up)
-    columns = out_weight.shape[1]
-    partial_value = jnp.dot(
-        lax.all_gather(head_out, "dp", axis=0, tiled=True),
-        out_weight,
-        preferred_element_type=jnp.float32,
-    )
-    summed = lax.psum_scatter(
-        partial_value.reshape(ranks, requests, columns).astype(jnp.bfloat16),
-        "tp",
-        scatter_dimension=1,
-        tiled=True,
-    )
-    landed = lax.all_to_all(summed, "dp", split_axis=0, concat_axis=2, tiled=True)
-    proj = landed.reshape(landed.shape[1], landed.shape[2])
-    stream = residual.astype(jnp.float32) + proj.astype(jnp.float32)
-    groups = [[2 * i, 2 * i + 1] for i in range(16)]
-    s16 = lax.all_to_all(
-        stream.reshape(8, 2, HALF), "dp", split_axis=1, concat_axis=0, axis_index_groups=groups, tiled=True
-    ).reshape(16, HALF)
-    owners = expert_owner[expert_ids]
-    picks = owners[:, :, None] == jnp.arange(ranks)[None, None, :]
-    shares = jnp.sum(jnp.where(picks, gate_weights[:, :, None], 0.0), axis=1)
-    shares = lax.all_gather(shares, ("dp", "tp"), axis=0, tiled=True)
-    coef = lax.dynamic_index_in_dim(shares, rank, 1, keepdims=False)
-    coef = coef.reshape(4, 4, 2, 4, 8).transpose(3, 0, 1, 2, 4).reshape(4, 4, 4, 16, 1)
-    coef = jnp.broadcast_to(coef, (4, 4, 4, 16, 128))
-    mixed = experts(s16, norm_gain, coef, w_gate, w_up, w_down)
-    return (mixed, arrived_blocks[None], arrived_scales[None])
+    mixed = experts(s16, norm_gain, expert_ids, gate_weights, expert_owner, w_gate, w_up, w_down)
+    return (mixed, blocks[None], scales[:, 0, 0][None])
 
 
 def solution(mesh):

time: 386 us -> 184 us (0.48)
  blocking collectives: 126 us -> 0 us
  Pallas kernels: 107 us -> 179 us
  waiting for transfers between devices: 57.5 us -> 0 us
  local copies, waits for them, and re-layouts: 43.8 us -> 3.6 us
  between operations: 19.3 us -> 0.66 us
  matrix products: 16.9 us -> 0 us
  starting transfers between devices: 7.9 us -> 0 us
  other arithmetic: 6.43 us -> 0 us
    pallas_call x0 -> x1, Pallas kernels: none -> 70.4 us  [attend_all(): pl.pallas_call(attend_kernel, out_shape=(jax.ShapeDtypeStruct((16, HALF),...]
    unnamed x1 -> x0, blocking collectives: 65.2 us -> none
    all_gather x1 -> x0, blocking collectives: 56.4 us -> none  [body(): shares = lax.all_gather(shares, ('dp', 'tp'), axis=0, tiled=True)]
    all_gather x2 -> x0, waiting for transfers between devices: 50.2 us -> none  [the longest x1 50.2 us: body(): lax.all_gather(head_out, 'dp', axis=0, tiled=True)]
    gather x6 -> x0, local copies, waits for them, and re-layouts: 19 us -> none  [the longest x1 11.7 us: attend(): cache_pool[block_table].reshape(requests, context, cache_pool.shape[2])]
    unnamed x35 -> x4, local copies, waits for them, and re-layouts: 21.1 us -> 2.28 us
    dot_general x3 -> x0, matrix products: 8.95 us -> none  [the longest x1 4.69 us: attend(): jnp.einsum('rhp,rpc->rhc', coef, tiles[:, :, :latent], preferred_element_...]
    sub x1 -> x0, matrix products: 7.93 us -> none  [attend(): expo = jnp.exp(scores - top)]
  transfers between devices with their start and end apart: 4 -> 0, of which waited for: 2 -> 0; matrix products, arithmetic and copies ran while one was open for 4% -> 0% of each run, Pallas kernels for 28% -> 0%
where the time goes in v2:
time: 184 us; the launch traced here: 183 us
  Pallas kernels  179 us (97%)
  local copies, waits for them, and re-layouts  3.6 us (2%)
    pallas_call x1, Pallas kernels, experts(): pl.pallas_call(expert_kernel, out_shape=jax.ShapeDtypeStruct((8, WIDE), b...  109 us
    pallas_call x1, Pallas kernels, attend_all(): pl.pallas_call(attend_kernel, out_shape=(jax.ShapeDtypeStruct((16, HALF),...  70.4 us

profile of v2, /device:TPU:1, one launch (start us, length us, event | category | flops | bytes accessed | tf_op | source)
XLA Modules:
  0.0 183.5 jit_solution(13261741167516788869)
XLA Ops:
  0.6 70.4 %attend.1 = (f32[16,3584]{1,0:T(8,128)}, bf16[4,64,576]{2,1,0:T(8,128)(2,1)}, bf16[4,16,128]{2,1,0:T(8,128)(2,1)}) custom-call(bf16[32,16,576]{2,1,0:T(8,128)(2,1)} %query.1, bf16[64,576,128]{2,1,0:T(8,128)(2,1)} %bitcast.8, s32[4,32]{1,0:T(4,128)} %bitcast.12, bf16[1,128]{1,0:T(2,128)(2,1)} %bitcast.14, s32[32]{0:T(128)} %lens_s.1, s32[3,16]{1,0:T(4,128)} %bitcast.13, ...), custom_call_target="tpu_custom_call" | custom-call | tf_op jit(solution)/shard_map/attend/pallas_call | solution.py:686
  71.1 0.0 copy-start
  71.1 108.8 %experts.1 = bf16[8,7168]{1,0:T(8,128)(2,1)} custom-call(f32[16,3584]{1,0:T(8,128)} %get-tuple-element.6.s16, f32[2,1,3584]{2,1,0:T(1,128)} %bitcast.11, s32[8,8]{1,0:T(8,128)} %ids.1, f32[8,8]{1,0:T(8,128)} %gates.1, s32[32]{0:T(128)} %owner.1, bf16[1,7168,256]{2,1,0:T(8,128)(2,1)} %wg_in.1, bf16[1,7168,256]{2,1,0:T(8,128)(2,1)} %wu_in.1, ...), custom_call_target="tpu_custom_call" | custom-call | tf_op jit(solution)/shard_map/experts/pallas_call | solution.py:353
  179.9 1.3 slice_reduce_fusion
  181.2 1.6 copy.21
  182.7 0.0 copy-done
  182.7 0.7 copy.22
Async XLA Ops:
  71.1 111.7 %copy-start = (bf16[4,64,576]{2,1,0:T(8,128)(2,1)S(1)}, bf16[4,64,576]{2,1,0:T(8,128)(2,1)}, u32[]{:S(2)}) copy-start(bf16[4,64,576]{2,1,0:T(8,128)(2,1)} %get-tuple-element.7) | copy-start | bytes 884740

commit v3 on v1

v3 whole, which is shorter than its diff:
```python
import functools
import jax
import jax.numpy as jnp
from jax import lax
from jax.experimental import pallas as pl
from jax.experimental.pallas import tpu as pltpu
from jax.sharding import PartitionSpec as P

MESH = pl.DeviceIdType.MESH
norm_eps = 1e-06
WIDE = 7168
HALF = 3584
PARTS = ((0, 1280), (1280, 1280), (2560, 1024))
GRIDS = (1280, 1280, 1152)
ORDER = ((0, 1, 2), (1, 2, 0), (2, 0, 1))
TILE = 256


class Links:
    def __init__(self, send, recv):
        self.send, self.recv, self.used = send, recv, 0
        rank = lax.axis_index("dp")
        self.core = lax.rem(rank, 2)
        self.pos = (lax.axis_index("tp"), rank // 8, lax.rem(rank // 2, 4))

    def device(self, pos, core):
        return ((pos[1] * 4 + pos[2]) * 2 + core, pos[0])

    def along(self, axis, step):
        return lax.rem(self.pos[axis] + step, 4)

    def near(self, axis, step):
        pos = list(self.pos)
        pos[axis] = self.along(axis, step)
        return self.device(pos, self.core)

    def twin(self):
        return self.device(self.pos, 1 - self.core)

    def copy(self, src, dst, device):
        slot = self.used
        self.used += 1
        made = pltpu.make_async_remote_copy(
            src_ref=src,
            dst_ref=dst,
            send_sem=self.send.at[slot],
            recv_sem=self.recv.at[slot],
            device_id=device,
            device_id_type=MESH,
        )
        made.start()
        return made


def place(part, a, b, c):
    index = [None, None, None]
    for axis, value in zip(ORDER[part], (a, b, c)):
        index[axis] = value
    return tuple(index)


ALL = slice(None)


softmax_scale = 192.0 ** (-0.5)
OWN = 224
WITHIN = (((0,), (0,)), ((), ()))
LAST = (((1,), (1,)), ((), ()))
MIG = ((0, 32, 1, 2), (32, 48, 2, 1))


def kernel(
    query, pool, table, scales, lens_s, mig_s, value_up, out_w, residual,
    gain, ids, gates, owner, wg_in, wu_in, wd_in,
    out, blocks_out, scales_out,
    x0, x1, x2, t0, t1, t2, wg, wu, wd, accg, accu, hid,
    r0, r1, r2, ca0, ca1, ca2, cb0, cb1, cb2, bb0, bb1, bb2, aa0, aa1, aa2,
    sums, both, fin,
    kt, hot, vu, wt, lat, h00, h01, h10, h11, n00, n01, n10, n11, part, px_, rx, sp, gx, res, mg, quarter, lane_scale, row, s16,
    load, send, recv, recv2, send2,
):
    keys_in = (t0, t1, r0, r1)
    net = Links(send, recv)
    core = net.core
    x, y, z = net.pos
    rank = (y * 4 + z) * 2 + core
    heads = ((h00, h01), (h10, h11))
    twin_heads = ((n00, n01), (n10, n11))
    f32, bf = jnp.float32, jnp.bfloat16

    def fetch(i, slot):
        return pltpu.make_async_copy(pool.at[pl.ds(i * 4, 4)], kt.at[slot], load.at[slot])

    for i in range(4):
        fetch(i, i).start()
    late = []
    for i, (src, dst) in enumerate(((value_up, vu), (out_w, wt.at[pl.ds(0, OWN)]))):
        made = pltpu.make_async_copy(src, dst, load.at[4 + i])
        made.start()
        late.append(made)

    barrier = pltpu.get_barrier_semaphore()
    for k in range(1, 32):
        other = lax.rem(rank + k, 32)
        pl.semaphore_signal(barrier, inc=1, device_id=(other, x), device_id_type=MESH)
    for k in range(1, 4):
        pl.semaphore_signal(barrier, inc=1, device_id=net.near(0, k), device_id_type=MESH)

    rows = lax.broadcasted_iota(jnp.int32, (32, 128), 0)
    widen = (rows == lax.broadcasted_iota(jnp.int32, (32, 128), 1) // 4).astype(f32)
    names = jnp.dot(table[...].astype(f32), widen, preferred_element_type=f32)
    held = lax.broadcasted_iota(jnp.int32, (4, 128), 0) == lax.rem(lax.broadcasted_iota(jnp.int32, (4, 128), 1), 4)
    names = jnp.sum(jnp.where(held, names, 0.0), axis=0, keepdims=True)
    names = jnp.broadcast_to(names, (128, 128))
    turned = (names == lax.broadcasted_iota(jnp.int32, (128, 128), 0).astype(f32)).astype(f32)
    hot[0:128] = turned.T.astype(bf)
    leaving, sender, has_in = 0, 0, 0
    for i in range(16):
        goes = mig_s[1, i] == rank
        leaving += jnp.where(goes, mig_s[0, i] - rank * 32, 0)
        comes = mig_s[2, i] == rank
        sender += jnp.where(comes, mig_s[1, i], 0)
        has_in += jnp.where(comes, 1, 0)
    slot = leaving * 4 + x
    only = lax.broadcasted_iota(jnp.int32, (128, 128), 0) == slot
    only = jnp.sum(jnp.where(only, hot[0:128].astype(f32), 0.0), axis=0, keepdims=True)
    hot[128:144] = jnp.broadcast_to(only, (16, 128)).astype(bf)
    slot_scale = jnp.dot(jnp.broadcast_to(scales[...].astype(f32), (16, 128)).astype(bf), turned.astype(bf), preferred_element_type=f32)[0:8]
    groups = lax.broadcasted_iota(jnp.int32, (8, 128), 0) == lax.broadcasted_iota(jnp.int32, (8, 128), 1) // 16
    spread = (
        lax.rem(lax.broadcasted_iota(jnp.int32, (128, 1024), 0), 16)
        == lax.rem(lax.broadcasted_iota(jnp.int32, (128, 1024), 1), 16)
    ).astype(bf)
    lane_scale[...] = jnp.dot(jnp.where(groups, slot_scale, 0.0).astype(bf), spread, preferred_element_type=f32).reshape(8, 1, 1024)
    wt[pl.ds(OWN, 32)] = jnp.zeros((32, 2048), bf)

    def turn(i, carry):
        slot = lax.rem(i, 4)
        fetch(i, slot).wait()
        for n in range(4):
            got = lax.dot_general(hot[...], kt[slot, n], LAST, preferred_element_type=f32)
            for g in range(8):
                keys_in[g // 2][i // 4, lax.rem(i, 4), n, :, (g % 2) * 640:(g % 2) * 640 + 576] = got[g * 16:(g + 1) * 16].astype(bf)
            row[pl.ds(i * 4 + n, 1)] = got[128:129]

        @pl.when(i < 12)
        def _():
            fetch(i + 4, slot).start()

        return carry

    lax.fori_loop(0, 16, turn, 0)
    loads = []
    for half in range(2):
        which = core if half == 0 else 1 - core
        rows = pl.ds(pl.multiple_of(which * HALF, HALF), HALF)
        for n, (src, dst) in enumerate(
            ((wg_in.at[0, rows, :], wg.at[half]), (wu_in.at[0, rows, :], wu.at[half]), (wd_in.at[0, :, rows], wd.at[half]))
        ):
            made = pltpu.make_async_copy(src, dst, load.at[6 + half * 3 + n])
            made.start()
            loads.append(made)

    its = jnp.sum(jnp.where(lax.broadcasted_iota(jnp.int32, (8, 128), 1) == slot, slot_scale, 0.0)[0:1], axis=1, keepdims=True)
    mg[core, y, z, 0:64] = row[...].astype(bf)
    mg[core, y, z, 64:80] = jnp.broadcast_to(its, (16, 576)).astype(bf)

    pl.semaphore_wait(barrier, 34)
    sent = []

    def go(src, dst, device):
        made = net.copy(src, dst, device)
        sent.append(made)
        return made

    mine = residual[:, pl.ds(pl.multiple_of(core * HALF, HALF), HALF)].astype(f32)
    rows = pl.ds(pl.multiple_of(core * 8, 8), 8)
    res[0, rows] = mine
    res[1, rows] = residual[:, pl.ds(pl.multiple_of((1 - core) * HALF, HALF), HALF)].astype(f32)
    swap = go(res.at[1, rows], res.at[0, rows], net.twin())

    def mig_line(i, first):
        off, n, a, b = MIG[i]
        r = pl.ds(off, n)
        return mg.at[core, first, :, r] if a == 2 else mg.at[core, :, first, r]

    m1 = []
    for off, n, a, b in MIG:
        src = mg.at[core, y, z, pl.ds(off, n)]
        m1.append([go(src, src, net.near(a, k)) for k in (1, 3, 2)])
    m2, mt = [None, None], []

    def mig_spread(i):
        off, n, a, b = MIG[i]
        for made in m1[i]:
            made.wait_recv()
        src = mig_line(i, net.pos[b])
        m2[i] = [go(src, src, net.near(b, k)) for k in (1, 3, 2)]
        mt.append(go(src, src, net.twin()))

    def mig_twin(i):
        b = MIG[i][3]
        for k, made in zip((1, 3, 2), m2[i]):
            made.wait_recv()
            src = mig_line(i, net.along(b, 4 - k))
            mt.append(go(src, src, net.twin()))

    def attend(b, k, carry):
        g = b * 2 + k
        q = query[pl.ds(g * 4, 4)].reshape(64, 576)
        keys = keys_in[b][:, :, :, :, pl.ds(pl.multiple_of(k * 640, 640), 576)].reshape(1024, 576)
        scale = lane_scale[g]
        score = lax.dot_general(q, keys, LAST, preferred_element_type=f32)
        lane = lax.broadcasted_iota(jnp.int32, (1, 1024), 1)
        which = lax.rem(lane, 16)
        owner = which // 4
        place_ = lax.rem(which, 4) * 64 + lane // 16
        limit = jnp.where(owner == 0, lens_s[g * 4], jnp.where(owner == 1, lens_s[g * 4 + 1], jnp.where(owner == 2, lens_s[g * 4 + 2], lens_s[g * 4 + 3])))
        holder = jnp.where(place_ < limit, owner, -1)
        live = holder == lax.broadcasted_iota(jnp.int32, (64, 1024), 0) // 16
        score = jnp.where(live, score * (scale * softmax_scale), -1e30)
        top = jnp.max(score, axis=1, keepdims=True)
        expo = jnp.exp(score - top)
        total = jnp.sum(expo, axis=1, keepdims=True)
        coef = (expo * (1.0 / total) * scale).astype(bf)
        got = jnp.dot(coef, keys[:, 0:512], preferred_element_type=f32)
        for n in range(4):
            lat[n, pl.ds(pl.multiple_of(g * 64, 64), 64)] = got[:, n * 128:(n + 1) * 128]
        return carry

    ga = [[None] * 2, [None] * 2]
    gb = [[None] * 2, [None] * 2]
    tw = [[[], []], [[], []]]
    AXES = ((1, 2), (2, 1))

    def value_map(half):
        for h in range(16):
            rows = [lat[n, pl.ds(half * 256 + h, 16, stride=16), :] for n in range(4)]
            rows = jnp.concatenate(rows, axis=1).astype(bf)
            got = jnp.dot(rows, vu[h], preferred_element_type=f32).astype(bf)
            heads[half][h // 8][y, z, :, (h % 8) * 128:(h % 8 + 1) * 128] = got

    def head_line(ref, p, first):
        return ref.at[:, first] if p == 0 else ref.at[first]

    def head_start(half):
        for p in range(2):
            src = heads[half][p].at[y, z]
            ga[half][p] = [go(src, src, net.near(AXES[p][0], k)) for k in (1, 3, 2)]

    def head_twin(half, p, first):
        tw[half][p].append(go(head_line(heads[half][p], p, first), head_line(twin_heads[half][p], p, first), net.twin()))

    def head_spread(half):
        for p in range(2):
            for made in ga[half][p]:
                made.wait_recv()
            first = net.pos[AXES[p][1]]
            src = head_line(heads[half][p], p, first)
            gb[half][p] = [go(src, src, net.near(AXES[p][1], k)) for k in (1, 3, 2)]
            head_twin(half, p, first)

    def head_finish(half):
        for i in range(3):
            for p in range(2):
                gb[half][p][i].wait_recv()
                head_twin(half, p, net.along(AXES[p][1], 4 - (1, 3, 2)[i]))

    def project(half, refs, who):
        def step(k, carry):
            total = lax.dot_general(refs[0][k].reshape(64, 1024), wt[:, 0:1024], LAST, preferred_element_type=f32)
            total += lax.dot_general(refs[1][k].reshape(64, 1024), wt[:, 1024:2048], LAST, preferred_element_type=f32)
            part[half, who, k] = total.reshape(4, 16, 256)
            return carry

        lax.fori_loop(0, 4, step, 0)

    lax.fori_loop(0, 2, functools.partial(attend, 0), 0)
    lax.fori_loop(0, 2, functools.partial(attend, 1), 0)
    for made in late:
        made.wait()
    value_map(0)
    head_start(0)
    lax.fori_loop(0, 2, functools.partial(attend, 2), 0)
    head_spread(0)
    lax.fori_loop(0, 2, functools.partial(attend, 3), 0)
    value_map(1)
    head_start(1)
    head_spread(1)
    head_finish(0)
    project(0, heads[0], core)
    for p in range(2):
        for made in tw[0][p]:
            made.wait_recv()
    project(0, twin_heads[0], 1 - core)

    def shares(half):
        for n in range(2):
            rows = pl.ds(n * 8, 8)
            both = jnp.concatenate([part[half, 0, :, :, rows], part[half, 1, :, :, rows]], axis=2)
            px_[half * 2 + n] = both.astype(bf)

    shares(0)
    head_finish(1)
    project(1, heads[1], core)
    for p in range(2):
        for made in tw[1][p]:
            made.wait_recv()
    project(1, twin_heads[1], 1 - core)
    shares(1)
    back = [go(px_.at[net.along(0, k)], rx.at[n], net.near(0, k)) for n, k in enumerate((1, 3, 2))]
    mig_spread(0)
    mig_spread(1)
    for made in back:
        made.wait_recv()

    def add(k, carry):
        total = px_[x, k].astype(f32)
        for n in range(3):
            total = total + rx[n, k].astype(f32)
        sp[k] = total.astype(bf)
        return carry

    lax.fori_loop(0, 4, add, 0)
    to_core = y // 2
    here = (lax.rem(y, 2) * 4 + z) * 2 + core
    away = []
    for k in range(16):
        ty, tz = net.along(1, k // 4), net.along(2, k % 4)
        made = pltpu.make_async_remote_copy(
            src_ref=sp.at[ty, tz], dst_ref=gx.at[here], send_sem=send2.at[k], recv_sem=recv2.at[here],
            device_id=net.device((x, ty, tz), to_core), device_id_type=MESH,
        )
        away.append(made)
        if k:
            made.start()

    @pl.when(to_core != core)
    def _():
        away[0].start()

    @pl.when(to_core == core)
    def _():
        gx[here] = sp[y, z]

    swap.wait_recv()
    for j in range(16):
        made = pltpu.make_async_remote_copy(
            src_ref=sp.at[0, 0], dst_ref=gx.at[j], send_sem=send2.at[j], recv_sem=recv2.at[j],
            device_id=net.twin(), device_id_type=MESH,
        )

        @pl.when(jnp.logical_or(to_core != core, here != j))
        def _():
            made.wait_recv()

        cols = slice(j * OWN, (j + 1) * OWN)
        s16[:, cols] = res[0, :, cols] + gx[j].astype(f32)[:, 0:OWN]
    for k in range(1, 16):
        away[k].wait_send()

    @pl.when(to_core != core)
    def _():
        away[0].wait_send()

    mig_twin(0)
    mig_twin(1)

    x, t, r = (x0, x1, x2), (t0, t1, t2), (r0, r1, r2)
    ca, cb, bb, aa = (ca0, ca1, ca2), (cb0, cb1, cb2), (bb0, bb1, bb2), (aa0, aa1, aa2)

    stream = s16[...]
    power = jnp.sum(stream * stream, axis=1, keepdims=True)
    sums[0, 0:16] = jnp.broadcast_to(power, (16, 128))
    lane = lax.broadcasted_iota(jnp.int32, (1, 128), 1)
    held = jnp.full((1, 128), -1, jnp.int32)
    for e in range(32):
        at = owner[e]
        held = jnp.where(jnp.logical_or(lane == at, lane == at + 32), e, held)
    share = jnp.zeros((8, 128), jnp.float32)
    for k in range(8):
        share = share + jnp.where(ids[:, k:k + 1] == held, gates[:, k:k + 1], 0.0)
    sums[0, 16:24] = share
    both[pl.ds(pl.multiple_of(core * 8, 8), 8)] = share
    pair = net.copy(sums.at[0], sums.at[1], net.twin())
    accg[...] = jnp.zeros_like(accg)
    accu[...] = jnp.zeros_like(accu)
    pair.wait()
    power = (sums[0, 0:16][:, 0:1] + sums[1, 0:16][:, 0:1]) * (1.0 / WIDE)
    scale = lax.rsqrt(power + norm_eps)
    both[pl.ds(pl.multiple_of((1 - core) * 8, 8), 8)] = sums[1, 16:24]
    share = both[...]
    high = share.astype(jnp.bfloat16)
    rest = (share - high.astype(jnp.float32)).astype(jnp.bfloat16)
    px, py, pz = net.pos
    x[2][px, py, pz, :, 1024:1152] = jnp.where(lane < 32, high, rest)
    for p, (off, width) in enumerate(PARTS):
        cols = slice(off, off + width)
        x[p][px, py, pz, :, 0:width] = (s16[:, cols] * scale * gain[core][:, cols]).astype(jnp.bfloat16)
    ga = []
    for p in range(3):
        block = x[p].at[px, py, pz]
        ga.append([go(block, block, net.near(ORDER[p][0], k)) for k in (1, 3, 2)])
    for made in mt:
        made.wait_recv()
    found = mg[lax.rem(sender, 2), sender // 8, lax.rem(sender // 2, 4)]
    quarter[px] = jnp.where(has_in > 0, found, jnp.zeros_like(found))
    mx = [go(quarter.at[px], quarter.at[px], net.near(0, k)) for k in (1, 3, 2)]

    JS = (0, 1, 3, 2)
    SLOT = {1: 1, 3: 0, 2: 2}
    gb = [None] * 3
    gc = [[None] * 4 for _ in range(3)]
    gf = [[None] * 4 for _ in range(3)]
    twins = []

    def line(p, ref, jb, jc):
        return ref.at[place(p, ALL, net.along(ORDER[p][1], jb), net.along(ORDER[p][2], jc))]

    def to_twin(p, jb, jc):
        made = go(line(p, x[p], jb, jc), line(p, t[p], jb, jc), net.twin())
        twins.append((p, jb, jc, made))

    def spread(p, n):
        src = line(p, x[p], JS[n], 0)
        gc[p][n] = [go(src, src, net.near(ORDER[p][2], k)) for k in (1, 3)]
        to_twin(p, JS[n], 0)

    def multiply(p, ref, jc, half):
        off, width = PARTS[p]
        where = place(p, ALL, ALL, net.along(ORDER[p][2], jc))

        def step(k, carry):
            lanes = pl.ds(pl.multiple_of(k * TILE, TILE), TILE)
            rows = pl.ds(pl.multiple_of(off + k * TILE, TILE), TILE)
            left = ref[where + (ALL, lanes)].reshape(256, TILE)
            accg[where] += jnp.dot(left, wg[half, rows, :], preferred_element_type=jnp.float32).reshape(4, 4, 16, 256)
            accu[where] += jnp.dot(left, wu[half, rows, :], preferred_element_type=jnp.float32).reshape(4, 4, 16, 256)
            return carry

        lax.fori_loop(0, width // TILE, step, 0)

    for p in range(3):
        for made in ga[p]:
            made.wait_recv()
        src = line(p, x[p], 0, 0)
        gb[p] = [go(src, src, net.near(ORDER[p][1], k)) for k in (1, 3, 2)]
        spread(p, 0)
    for made in loads:
        made.wait()
    for n in (1, 2, 3):
        for p in range(3):
            gb[p][SLOT[JS[n]]].wait_recv()
            spread(p, n)
    for n in range(4):
        for p in range(3):
            gc[p][n][0].wait_recv()
            gc[p][n][1].wait_recv()
            if n % 2 == 0:
                src = line(p, x[p], JS[n], 3)
                gf[p][n] = go(src, src, net.near(ORDER[p][2], 1))
            else:
                src = line(p, x[p], JS[n], 1)
                gf[p][n] = go(src, src, net.near(ORDER[p][2], 3))
            to_twin(p, JS[n], 3)
            to_twin(p, JS[n], 1)
            if n == 0:
                multiply(p, x[p], 0, 0)
            if n == 1:
                for q, jb, jc, made in twins:
                    if q == p and jc == 0:
                        made.wait_recv()
                multiply(p, t[p], 0, 1)
    for p in range(3):
        multiply(p, x[p], 1, 0)
        multiply(p, x[p], 3, 0)
        for jc in (1, 3):
            for q, jb, kc, made in twins:
                if q == p and kc == jc:
                    made.wait_recv()
            multiply(p, t[p], jc, 1)
    for p in range(3):
        for n in range(4):
            gf[p][n].wait_recv()
            to_twin(p, JS[n], 2)
        multiply(p, x[p], 2, 0)
    for p in range(3):
        for q, jb, kc, made in twins:
            if q == p and kc == 2:
                made.wait_recv()
        multiply(p, t[p], 2, 1)
    for made in sent:
        made.wait_send()
    sent.clear()

    for made in mx:
        made.wait_recv()
    for i in range(4):
        blocks_out[i] = quarter[i, 0:64]
        scales_out[i] = quarter[i, 64:80, 0:128]
    mine = jnp.logical_or(lane == rank, lane == rank + 32)

    def activate(k, carry):
        g = accg[k].reshape(256, 256)
        u = accu[k].reshape(256, 256)
        c = x[2][k, :, :, :, 1024:1152].reshape(256, 128).astype(jnp.float32)
        c = jnp.sum(jnp.where(mine, c, 0.0), axis=1, keepdims=True)
        hid[k] = (g * jax.nn.sigmoid(g) * u * c).astype(jnp.bfloat16).reshape(4, 4, 16, 256)
        return carry

    lax.fori_loop(0, 4, activate, 0)

    def down_twin(p, jc):
        off, width = PARTS[p]
        where = place(p, ALL, ALL, net.along(ORDER[p][2], jc))

        def step(k, carry):
            lanes = pl.ds(pl.multiple_of(k * TILE, TILE), TILE)
            cols = pl.ds(pl.multiple_of(off + k * TILE, TILE), TILE)
            got = jnp.dot(hid[where].reshape(256, 256), wd[1, :, cols], preferred_element_type=jnp.float32)
            t[p][where + (ALL, lanes)] = got.astype(jnp.bfloat16).reshape(4, 4, 16, TILE)
            return carry

        lax.fori_loop(0, width // TILE, step, 0)
        return go(t[p].at[where + (ALL, pl.ds(0, width))], r[p].at[where], net.twin())

    def down_own(p, jc, made):
        off, width = PARTS[p]
        where = place(p, ALL, ALL, net.along(ORDER[p][2], jc))
        made.wait_recv()

        def step(k, carry):
            lanes = pl.ds(pl.multiple_of(k * TILE, TILE), TILE)
            cols = pl.ds(pl.multiple_of(off + k * TILE, TILE), TILE)
            got = jnp.dot(hid[where].reshape(256, 256), wd[0, :, cols], preferred_element_type=jnp.float32)
            got = got + r[p][where + (ALL, lanes)].reshape(256, TILE).astype(jnp.float32)
            x[p][where + (ALL, lanes)] = got.astype(jnp.bfloat16).reshape(4, 4, 16, TILE)
            return carry

        lax.fori_loop(0, width // TILE, step, 0)

    JB = (2, 1, 3, 0)
    PLUS, MINUS = (0, 3), (1, 2)
    steps = [(p, jc) for jc in (2, 1, 3, 0) for p in range(3)]
    made_twin = {}
    h1, h2 = {}, {}

    def add_line(p, jb, jc, others):
        b, c = net.along(ORDER[p][1], jb), net.along(ORDER[p][2], jc)

        def step(k, carry):
            where = place(p, k, b, c) + (ALL, pl.ds(0, PARTS[p][1]))
            total = x[p][where].astype(jnp.float32)
            for ref, index in others:
                total = total + ref[index + (k,)].astype(jnp.float32)
            x[p][where] = total.astype(jnp.bfloat16)
            return carry

        lax.fori_loop(0, 4, step, 0)

    def out_line(p, jb, jc):
        where = place(p, ALL, net.along(ORDER[p][1], jb), net.along(ORDER[p][2], jc))
        return x[p].at[where + (ALL, pl.ds(0, PARTS[p][1]))]

    def send_c1(p):
        h1[p] = []
        for i, n in enumerate(PLUS):
            h1[p].append(go(out_line(p, JB[n], 2), ca[p].at[0, i], net.near(ORDER[p][2], 1)))
        for i, n in enumerate(MINUS):
            h1[p].append(go(out_line(p, JB[n], 2), ca[p].at[1, i], net.near(ORDER[p][2], 3)))

    def send_c2(p, jc):
        way = 0 if jc == 1 else 1
        mine = PLUS if jc == 1 else MINUS
        for i in range(2):
            h1[p][way * 2 + i].wait_recv()
        for n in range(4):
            if n in mine:
                add_line(p, JB[n], jc, [(ca[p], (way, mine.index(n)))])
            h2[p, way, n] = go(out_line(p, JB[n], jc), cb[p].at[way, n], net.near(ORDER[p][2], jc))

    made_twin[steps[0]] = down_twin(*steps[0])
    for i, (p, jc) in enumerate(steps):
        if i + 1 < len(steps):
            made_twin[steps[i + 1]] = down_twin(*steps[i + 1])
        down_own(p, jc, made_twin[p, jc])
        if jc == 2:
            send_c1(p)
        elif jc != 0:
            send_c2(p, jc)
    hb = [[None] * 4 for _ in range(3)]
    for n in range(3):
        for p in range(3):
            for way in range(2):
                h2[p, way, n].wait_recv()
            add_line(p, JB[n], 0, [(cb[p], (0, n)), (cb[p], (1, n))])
            hb[p][n] = go(out_line(p, JB[n], 0), bb[p].at[n], net.near(ORDER[p][1], JB[n]))
    for p in range(3):
        for way in range(2):
            h2[p, way, 3].wait_recv()
        for n in range(3):
            hb[p][n].wait_recv()
        add_line(p, 0, 0, [(cb[p], (0, 3)), (cb[p], (1, 3))] + [(bb[p], (n,)) for n in range(3)])
    haa = []
    for p in range(3):
        _, mb, mc = (net.pos[axis] for axis in ORDER[p])
        for n, k in enumerate((2, 1, 3)):
            src = x[p].at[place(p, net.along(ORDER[p][0], k), mb, mc) + (ALL, pl.ds(0, PARTS[p][1]))]
            haa.append(go(src, aa[p].at[n], net.near(ORDER[p][0], k)))
    for p, (off, width) in enumerate(PARTS):
        for n in range(3):
            haa[p * 3 + n].wait_recv()
        total = x[p][px, py, pz, :, 0:width].astype(jnp.float32)
        for n in range(3):
            total = total + aa[p][n].astype(jnp.float32)
        fin[0, :, off:off + width] = s16[:, off:off + width] + total
    theirs = fin.at[0, pl.ds(pl.multiple_of((1 - core) * 8, 8), 8)]
    last = net.copy(theirs, fin.at[1, pl.ds(0, 8)], net.twin())
    mine = fin[0, pl.ds(pl.multiple_of(core * 8, 8), 8)]
    out[:, pl.ds(pl.multiple_of(core * HALF, HALF), HALF)] = mine.astype(jnp.bfloat16)
    last.wait_recv()
    out[:, pl.ds(pl.multiple_of((1 - core) * HALF, HALF), HALF)] = fin[1, 0:8].astype(jnp.bfloat16)
    last.wait_send()
    for made in sent:
        made.wait_send()


def layer(
    query, pool, block_scale, table, lengths, migration, value_up, out_weight, residual,
    gain, ids, gates, owner, w_gate, w_up, w_down,
):
    bf, f32 = jnp.bfloat16, jnp.float32
    vm = pl.BlockSpec(memory_space=pltpu.VMEM)
    sm = pl.BlockSpec(memory_space=pltpu.SMEM)
    hbm = pl.BlockSpec(memory_space=pl.ANY)
    head = [pltpu.VMEM((4, 4, 16, 1024), bf)] * 8
    grid = [pltpu.VMEM((4, 4, 4, 16, w), bf) for w in GRIDS]
    slots = 250
    return pl.pallas_call(
        kernel,
        out_shape=(
            jax.ShapeDtypeStruct((8, WIDE), bf),
            jax.ShapeDtypeStruct((4, 64, 576), bf),
            jax.ShapeDtypeStruct((4, 16, 128), bf),
        ),
        in_specs=[vm, hbm, vm, vm, sm, sm, hbm, hbm, vm, vm, vm, vm, sm, hbm, hbm, hbm],
        out_specs=(vm, vm, vm),
        scratch_shapes=grid + grid + [
            pltpu.VMEM((2, HALF, 256), bf),
            pltpu.VMEM((2, HALF, 256), bf),
            pltpu.VMEM((2, 256, HALF), bf),
            pltpu.VMEM((4, 4, 4, 16, 256), f32),
            pltpu.VMEM((4, 4, 4, 16, 256), f32),
            pltpu.VMEM((4, 4, 4, 16, 256), bf),
        ] + [pltpu.VMEM((4, 4, 4, 16, w), bf) for _, w in PARTS]
        + [pltpu.VMEM((2, 2, 4, 16, w), bf) for _, w in PARTS]
        + [pltpu.VMEM((2, 4, 4, 16, w), bf) for _, w in PARTS]
        + [pltpu.VMEM((3, 4, 16, w), bf) for _, w in PARTS]
        + [pltpu.VMEM((3, 16, w), bf) for _, w in PARTS]
        + [
            pltpu.VMEM((2, 24, 128), f32),
            pltpu.VMEM((16, 128), f32),
            pltpu.VMEM((2, 16, HALF), f32),
            pltpu.VMEM((4, 4, 576, 128), bf),
            pltpu.VMEM((144, 128), bf),
            pltpu.VMEM((16, 512, 128), bf),
            pltpu.VMEM((256, 2048), bf),
            pltpu.VMEM((4, 512, 128), f32),
        ] + head + [
            pltpu.VMEM((2, 2, 4, 4, 16, 256), f32),
            pltpu.VMEM((4, 4, 4, 16, 256), bf),
            pltpu.VMEM((3, 4, 4, 16, 256), bf),
            pltpu.VMEM((4, 4, 16, 256), bf),
            pltpu.VMEM((16, 16, 256), bf),
            pltpu.VMEM((2, 16, HALF), f32),
            pltpu.VMEM((2, 4, 4, 80, 576), bf),
            pltpu.VMEM((4, 80, 576), bf),
            pltpu.VMEM((8, 1, 1024), f32),
            pltpu.VMEM((64, 576), f32),
            pltpu.VMEM((16, HALF), f32),
            pltpu.SemaphoreType.DMA((12,)),
            pltpu.SemaphoreType.DMA((slots,)),
            pltpu.SemaphoreType.DMA((slots,)),
            pltpu.SemaphoreType.DMA((16,)),
            pltpu.SemaphoreType.DMA((16,)),
        ],
        compiler_params=pltpu.CompilerParams(collective_id=1, has_side_effects=True, vmem_limit_bytes=63 * 2**20),
        name="layer",
    )(
        query, jnp.transpose(pool, (1, 2, 0)), table.T, block_scale.reshape(1, 128), lengths,
        migration.T, value_up, out_weight.T, residual,
        gain.reshape(2, 1, HALF), ids, gates, owner, w_gate, w_up, w_down,
    )


def body(
    query, cache_pool, block_scale, block_table, lengths, migration, value_up, out_weight, residual, norm_gain,
    expert_ids, gate_weights, expert_owner, w_gate, w_up, w_down,
):
    mixed, blocks, scales = layer(
        query, cache_pool, block_scale, block_table, lengths, migration, value_up, out_weight, residual,
        norm_gain, expert_ids, gate_weights, expert_owner, w_gate, w_up, w_down,
    )
    return (mixed, blocks[None], scales[:, 0, 0][None])


def solution(mesh):
    return jax.shard_map(
        body,
        mesh=mesh,
        in_specs=(
            P("dp", "tp", None),
            P("dp", None, None),
            P("dp"),
            P("dp", None),
            P("dp"),
            P(),
            P("tp", None, None),
            P("tp", "dp"),
            P(("dp", "tp"), None),
            P(),
            P(("dp", "tp"), None),
            P(("dp", "tp"), None),
            P(),
            P("dp", None, "tp"),
            P("dp", None, "tp"),
            P("dp", "tp", None),
        ),
        out_specs=(P(("dp", "tp"), None), P("dp", None, None, None), P("dp", None)),
        check_vma=False,
    )
```

time: 386 us -> 173 us (0.45)
  blocking collectives: 126 us -> 0 us
  Pallas kernels: 107 us -> 167 us
  waiting for transfers between devices: 57.5 us -> 0 us
  local copies, waits for them, and re-layouts: 43.8 us -> 4.6 us
  between operations: 19.3 us -> 0.65 us
  matrix products: 16.9 us -> 0 us
  starting transfers between devices: 7.9 us -> 0 us
  other arithmetic: 6.43 us -> 0 us
    unnamed x1 -> x0, blocking collectives: 65.2 us -> none
    pallas_call x1, Pallas kernels: 107 us -> 167 us  [layer(): pl.pallas_call(kernel, out_shape=(jax.ShapeDtypeStruct((8, WIDE), bf), ja...]
    all_gather x1 -> x0, blocking collectives: 56.4 us -> none  [body(): shares = lax.all_gather(shares, ('dp', 'tp'), axis=0, tiled=True)]
    all_gather x2 -> x0, waiting for transfers between devices: 50.2 us -> none  [the longest x1 50.2 us: body(): lax.all_gather(head_out, 'dp', axis=0, tiled=True)]
    gather x6 -> x0, local copies, waits for them, and re-layouts: 19 us -> none  [the longest x1 11.7 us: attend(): cache_pool[block_table].reshape(requests, context, cache_pool.shape[2])]
    unnamed x35 -> x2, local copies, waits for them, and re-layouts: 21.1 us -> 3.27 us
    dot_general x3 -> x0, matrix products: 8.95 us -> none  [the longest x1 4.69 us: attend(): jnp.einsum('rhp,rpc->rhc', coef, tiles[:, :, :latent], preferred_element_...]
    sub x1 -> x0, matrix products: 7.93 us -> none  [attend(): expo = jnp.exp(scores - top)]
  transfers between devices with their start and end apart: 4 -> 0, of which waited for: 2 -> 0; matrix products, arithmetic and copies ran while one was open for 4% -> 0% of each run, Pallas kernels for 28% -> 0%
where the time goes in v3:
time: 173 us; the launch traced here: 172 us
  Pallas kernels  167 us (97%)
  local copies, waits for them, and re-layouts  4.6 us (3%)
    pallas_call x1, Pallas kernels, layer(): pl.pallas_call(kernel, out_shape=(jax.ShapeDtypeStruct((8, WIDE), bf), ja...  167 us

profile of v3, /device:TPU:1, one launch (start us, length us, event | category | flops | bytes accessed | tf_op | source)
XLA Modules:
  0.0 172.3 jit_solution(2214783305611513052)
XLA Ops:
  0.6 167.0 %layer.1 = (bf16[8,7168]{1,0:T(8,128)(2,1)}, bf16[4,64,576]{2,1,0:T(8,128)(2,1)}, bf16[4,16,128]{2,1,0:T(8,128)(2,1)}) custom-call(bf16[32,16,576]{2,1,0:T(8,128)(2,1)} %query.1, bf16[64,576,128]{2,1,0:T(8,128)(2,1)} %bitcast.8, s32[4,32]{1,0:T(4,128)} %bitcast.12, bf16[1,128]{1,0:T(2,128)(2,1)} %bitcast.14, s32[32]{0:T(128)} %lens_s.1, s32[3,16]{1,0:T(4,128)} %bitcast.13, ...), custom_call_target="tpu_custom_call" | custom-call | tf_op jit(solution)/shard_map/layer/pallas_call | solution.py:639
  167.7 1.3 slice_reduce_fusion
  169.0 1.6 copy.21
  170.6 1.7 %copy.22 = bf16[1,4,64,576]{3,2,1,0:T(8,128)(2,1)} copy(bf16[1,4,64,576]{3,2,1,0:T(8,128)(2,1)} %bitcast.10) | data formatting | bytes 589824

commit v4 on v3

--- a/solution.py
+++ b/solution.py
@@ -13,7 +13,6 @@
 PARTS = ((0, 1280), (1280, 1280), (2560, 1024))
 GRIDS = (1280, 1280, 1152)
 ORDER = ((0, 1, 2), (1, 2, 0), (2, 0, 1))
-TILE = 256
 
 
 class Links:
@@ -66,7 +65,7 @@
 OWN = 224
 WITHIN = (((0,), (0,)), ((), ()))
 LAST = (((1,), (1,)), ((), ()))
-MIG = ((0, 32, 1, 2), (32, 48, 2, 1))
+MIG = ((0, 32, 1, 2), (32, 32, 2, 1))
 
 
 def kernel(
@@ -75,7 +74,7 @@
     out, blocks_out, scales_out,
     x0, x1, x2, t0, t1, t2, wg, wu, wd, accg, accu, hid,
     r0, r1, r2, ca0, ca1, ca2, cb0, cb1, cb2, bb0, bb1, bb2, aa0, aa1, aa2,
-    sums, both, fin,
+    both, fin,
     kt, hot, vu, wt, lat, h00, h01, h10, h11, n00, n01, n10, n11, part, px_, rx, sp, gx, res, mg, quarter, lane_scale, row, s16,
     load, send, recv, recv2, send2,
 ):
@@ -133,6 +132,18 @@
     ).astype(bf)
     lane_scale[...] = jnp.dot(jnp.where(groups, slot_scale, 0.0).astype(bf), spread, preferred_element_type=f32).reshape(8, 1, 1024)
     wt[pl.ds(OWN, 32)] = jnp.zeros((32, 2048), bf)
+    accg[...] = jnp.zeros_like(accg)
+    accu[...] = jnp.zeros_like(accu)
+    lane = lax.broadcasted_iota(jnp.int32, (1, 128), 1)
+    held = jnp.full((1, 128), -1, jnp.int32)
+    for e in range(32):
+        at = owner[e]
+        held = jnp.where(jnp.logical_or(lane == at, lane == at + 32), e, held)
+    share = jnp.zeros((8, 128), f32)
+    for k in range(8):
+        share = share + jnp.where(ids[:, k:k + 1] == held, gates[:, k:k + 1], 0.0)
+    both[pl.ds(pl.multiple_of(core * 8, 8), 8)] = share
+    both[pl.ds(pl.multiple_of((1 - core) * 8, 8), 8)] = jnp.zeros((8, 128), f32)
 
     def turn(i, carry):
         slot = lax.rem(i, 4)
@@ -162,8 +173,8 @@
             loads.append(made)
 
     its = jnp.sum(jnp.where(lax.broadcasted_iota(jnp.int32, (8, 128), 1) == slot, slot_scale, 0.0)[0:1], axis=1, keepdims=True)
-    mg[core, y, z, 0:64] = row[...].astype(bf)
-    mg[core, y, z, 64:80] = jnp.broadcast_to(its, (16, 576)).astype(bf)
+    mg[core, y, z, :, 0:576] = row[...].astype(bf)
+    mg[core, y, z, :, 576:640] = jnp.broadcast_to(its, (64, 64)).astype(bf)
 
     pl.semaphore_wait(barrier, 34)
     sent = []
@@ -267,13 +278,9 @@
                 head_twin(half, p, net.along(AXES[p][1], 4 - (1, 3, 2)[i]))
 
     def project(half, refs, who):
-        def step(k, carry):
-            total = lax.dot_general(refs[0][k].reshape(64, 1024), wt[:, 0:1024], LAST, preferred_element_type=f32)
-            total += lax.dot_general(refs[1][k].reshape(64, 1024), wt[:, 1024:2048], LAST, preferred_element_type=f32)
-            part[half, who, k] = total.reshape(4, 16, 256)
-            return carry
-
-        lax.fori_loop(0, 4, step, 0)
+        total = lax.dot_general(refs[0][...].reshape(256, 1024), wt[:, 0:1024], LAST, preferred_element_type=f32)
+        total += lax.dot_general(refs[1][...].reshape(256, 1024), wt[:, 1024:2048], LAST, preferred_element_type=f32)
+        part[half, who] = total.reshape(4, 4, 16, 256)
 
     lax.fori_loop(0, 2, functools.partial(attend, 0), 0)
     lax.fori_loop(0, 2, functools.partial(attend, 1), 0)
@@ -282,10 +289,10 @@
     value_map(0)
     head_start(0)
     lax.fori_loop(0, 2, functools.partial(attend, 2), 0)
-    head_spread(0)
     lax.fori_loop(0, 2, functools.partial(attend, 3), 0)
     value_map(1)
     head_start(1)
+    head_spread(0)
     head_spread(1)
     head_finish(0)
     project(0, heads[0], core)
@@ -314,14 +321,10 @@
     for made in back:
         made.wait_recv()
 
-    def add(k, carry):
-        total = px_[x, k].astype(f32)
-        for n in range(3):
-            total = total + rx[n, k].astype(f32)
-        sp[k] = total.astype(bf)
-        return carry
-
-    lax.fori_loop(0, 4, add, 0)
+    total = px_[x].astype(f32)
+    for n in range(3):
+        total = total + rx[n].astype(f32)
+    sp[...] = total.astype(bf)
     to_core = y // 2
     here = (lax.rem(y, 2) * 4 + z) * 2 + core
     away = []
@@ -371,32 +374,21 @@
 
     stream = s16[...]
     power = jnp.sum(stream * stream, axis=1, keepdims=True)
-    sums[0, 0:16] = jnp.broadcast_to(power, (16, 128))
     lane = lax.broadcasted_iota(jnp.int32, (1, 128), 1)
-    held = jnp.full((1, 128), -1, jnp.int32)
-    for e in range(32):
-        at = owner[e]
-        held = jnp.where(jnp.logical_or(lane == at, lane == at + 32), e, held)
-    share = jnp.zeros((8, 128), jnp.float32)
-    for k in range(8):
-        share = share + jnp.where(ids[:, k:k + 1] == held, gates[:, k:k + 1], 0.0)
-    sums[0, 16:24] = share
-    both[pl.ds(pl.multiple_of(core * 8, 8), 8)] = share
-    pair = net.copy(sums.at[0], sums.at[1], net.twin())
-    accg[...] = jnp.zeros_like(accg)
-    accu[...] = jnp.zeros_like(accu)
-    pair.wait()
-    power = (sums[0, 0:16][:, 0:1] + sums[1, 0:16][:, 0:1]) * (1.0 / WIDE)
-    scale = lax.rsqrt(power + norm_eps)
-    both[pl.ds(pl.multiple_of((1 - core) * 8, 8), 8)] = sums[1, 16:24]
-    share = both[...]
-    high = share.astype(jnp.bfloat16)
-    rest = (share - high.astype(jnp.float32)).astype(jnp.bfloat16)
     px, py, pz = net.pos
-    x[2][px, py, pz, :, 1024:1152] = jnp.where(lane < 32, high, rest)
     for p, (off, width) in enumerate(PARTS):
         cols = slice(off, off + width)
-        x[p][px, py, pz, :, 0:width] = (s16[:, cols] * scale * gain[core][:, cols]).astype(jnp.bfloat16)
+        x[p][px, py, pz, :, 0:width] = (s16[:, cols] * gain[core][:, cols]).astype(jnp.bfloat16)
+    every = both[...]
+    first = every.astype(jnp.bfloat16)
+    rest = (every - first.astype(jnp.float32)).astype(jnp.bfloat16)
+    tops = power.astype(jnp.bfloat16)
+    left = power - tops.astype(jnp.float32)
+    mids = left.astype(jnp.bfloat16)
+    lows = (left - mids.astype(jnp.float32)).astype(jnp.bfloat16)
+    extra = jnp.where(lane < 32, first, rest)
+    extra = jnp.where(lane == 64, tops, jnp.where(lane == 65, mids, jnp.where(lane == 66, lows, extra)))
+    x[2][px, py, pz, :, 1024:1152] = extra
     ga = []
     for p in range(3):
         block = x[p].at[px, py, pz]
@@ -408,7 +400,6 @@
     mx = [go(quarter.at[px], quarter.at[px], net.near(0, k)) for k in (1, 3, 2)]
 
     JS = (0, 1, 3, 2)
-    SLOT = {1: 1, 3: 0, 2: 2}
     gb = [None] * 3
     gc = [[None] * 4 for _ in range(3)]
     gf = [[None] * 4 for _ in range(3)]
@@ -430,28 +421,30 @@
         off, width = PARTS[p]
         where = place(p, ALL, ALL, net.along(ORDER[p][2], jc))
 
-        def step(k, carry):
-            lanes = pl.ds(pl.multiple_of(k * TILE, TILE), TILE)
-            rows = pl.ds(pl.multiple_of(off + k * TILE, TILE), TILE)
-            left = ref[where + (ALL, lanes)].reshape(256, TILE)
-            accg[where] += jnp.dot(left, wg[half, rows, :], preferred_element_type=jnp.float32).reshape(4, 4, 16, 256)
-            accu[where] += jnp.dot(left, wu[half, rows, :], preferred_element_type=jnp.float32).reshape(4, 4, 16, 256)
-            return carry
-
-        lax.fori_loop(0, width // TILE, step, 0)
+        left = ref[where + (ALL, pl.ds(0, width))].reshape(256, width)
+        accg[where] += jnp.dot(left, wg[half, off:off + width, :], preferred_element_type=jnp.float32).reshape(4, 4, 16, 256)
+        accu[where] += jnp.dot(left, wu[half, off:off + width, :], preferred_element_type=jnp.float32).reshape(4, 4, 16, 256)
 
     for p in range(3):
         for made in ga[p]:
             made.wait_recv()
         src = line(p, x[p], 0, 0)
-        gb[p] = [go(src, src, net.near(ORDER[p][1], k)) for k in (1, 3, 2)]
+        gb[p] = [go(src, src, net.near(ORDER[p][1], k)) for k in (1, 3)]
+    for p in range(3):
         spread(p, 0)
     for made in loads:
         made.wait()
-    for n in (1, 2, 3):
-        for p in range(3):
-            gb[p][SLOT[JS[n]]].wait_recv()
-            spread(p, n)
+    for p in range(3):
+        for k, jb, span in ((3, 1, pl.ds(2, 2)), (1, 3, pl.ds(0, 2))):
+            gb[p][0 if k == 1 else 1].wait_recv()
+            src = x[p].at[place(p, span, net.along(ORDER[p][1], jb), net.along(ORDER[p][2], 0))]
+            gb[p].append(go(src, src, net.near(ORDER[p][1], k)))
+        spread(p, 1)
+        spread(p, 2)
+    for p in range(3):
+        for made in gb[p][2:]:
+            made.wait_recv()
+        spread(p, 3)
     for n in range(4):
         for p in range(3):
             gc[p][n][0].wait_recv()
@@ -496,15 +489,22 @@
     for made in mx:
         made.wait_recv()
     for i in range(4):
-        blocks_out[i] = quarter[i, 0:64]
-        scales_out[i] = quarter[i, 64:80, 0:128]
+        blocks_out[i] = quarter[i, :, 0:576]
+        scales_out[i] = quarter[i, 0:16, 512:640]
     mine = jnp.logical_or(lane == rank, lane == rank + 32)
+
+    powers = jnp.logical_and(lane >= 64, lane < 67)
 
     def activate(k, carry):
         g = accg[k].reshape(256, 256)
         u = accu[k].reshape(256, 256)
-        c = x[2][k, :, :, :, 1024:1152].reshape(256, 128).astype(jnp.float32)
+        c = x[2][k, :, :, :, 1024:1152].astype(jnp.float32) + t[2][k, :, :, :, 1024:1152].astype(jnp.float32)
+        c = c.reshape(256, 128)
+        power = jnp.sum(jnp.where(powers, c, 0.0), axis=1, keepdims=True) * (1.0 / WIDE)
+        scale = lax.rsqrt(power + norm_eps)
         c = jnp.sum(jnp.where(mine, c, 0.0), axis=1, keepdims=True)
+        g = g * scale
+        u = u * scale
         hid[k] = (g * jax.nn.sigmoid(g) * u * c).astype(jnp.bfloat16).reshape(4, 4, 16, 256)
         return carry
 
@@ -513,31 +513,17 @@
     def down_twin(p, jc):
         off, width = PARTS[p]
         where = place(p, ALL, ALL, net.along(ORDER[p][2], jc))
-
-        def step(k, carry):
-            lanes = pl.ds(pl.multiple_of(k * TILE, TILE), TILE)
-            cols = pl.ds(pl.multiple_of(off + k * TILE, TILE), TILE)
-            got = jnp.dot(hid[where].reshape(256, 256), wd[1, :, cols], preferred_element_type=jnp.float32)
-            t[p][where + (ALL, lanes)] = got.astype(jnp.bfloat16).reshape(4, 4, 16, TILE)
-            return carry
-
-        lax.fori_loop(0, width // TILE, step, 0)
+        got = jnp.dot(hid[where].reshape(256, 256), wd[1, :, off:off + width], preferred_element_type=jnp.float32)
+        t[p][where + (ALL, pl.ds(0, width))] = got.astype(jnp.bfloat16).reshape(4, 4, 16, width)
         return go(t[p].at[where + (ALL, pl.ds(0, width))], r[p].at[where], net.twin())
 
     def down_own(p, jc, made):
         off, width = PARTS[p]
         where = place(p, ALL, ALL, net.along(ORDER[p][2], jc))
         made.wait_recv()
-
-        def step(k, carry):
-            lanes = pl.ds(pl.multiple_of(k * TILE, TILE), TILE)
-            cols = pl.ds(pl.multiple_of(off + k * TILE, TILE), TILE)
-            got = jnp.dot(hid[where].reshape(256, 256), wd[0, :, cols], preferred_element_type=jnp.float32)
-            got = got + r[p][where + (ALL, lanes)].reshape(256, TILE).astype(jnp.float32)
-            x[p][where + (ALL, lanes)] = got.astype(jnp.bfloat16).reshape(4, 4, 16, TILE)
-            return carry
-
-        lax.fori_loop(0, width // TILE, step, 0)
+        got = jnp.dot(hid[where].reshape(256, 256), wd[0, :, off:off + width], preferred_element_type=jnp.float32)
+        got = got + r[p][where].reshape(256, width).astype(jnp.float32)
+        x[p][where + (ALL, pl.ds(0, width))] = got.astype(jnp.bfloat16).reshape(4, 4, 16, width)
 
     JB = (2, 1, 3, 0)
     PLUS, MINUS = (0, 3), (1, 2)
@@ -547,16 +533,11 @@
 
     def add_line(p, jb, jc, others):
         b, c = net.along(ORDER[p][1], jb), net.along(ORDER[p][2], jc)
-
-        def step(k, carry):
-            where = place(p, k, b, c) + (ALL, pl.ds(0, PARTS[p][1]))
-            total = x[p][where].astype(jnp.float32)
-            for ref, index in others:
-                total = total + ref[index + (k,)].astype(jnp.float32)
-            x[p][where] = total.astype(jnp.bfloat16)
-            return carry
-
-        lax.fori_loop(0, 4, step, 0)
+        where = place(p, ALL, b, c) + (ALL, pl.ds(0, PARTS[p][1]))
+        total = x[p][where].astype(jnp.float32)
+        for ref, index in others:
+            total = total + ref[index].astype(jnp.float32)
+        x[p][where] = total.astype(jnp.bfloat16)
 
     def out_line(p, jb, jc):
         where = place(p, ALL, net.along(ORDER[p][1], jb), net.along(ORDER[p][2], jc))
@@ -569,15 +550,17 @@
         for i, n in enumerate(MINUS):
             h1[p].append(go(out_line(p, JB[n], 2), ca[p].at[1, i], net.near(ORDER[p][2], 3)))
 
-    def send_c2(p, jc):
+    def send_c2(p, jc, arrived):
         way = 0 if jc == 1 else 1
         mine = PLUS if jc == 1 else MINUS
-        for i in range(2):
-            h1[p][way * 2 + i].wait_recv()
+        if arrived:
+            for i in range(2):
+                h1[p][way * 2 + i].wait_recv()
         for n in range(4):
-            if n in mine:
-                add_line(p, JB[n], jc, [(ca[p], (way, mine.index(n)))])
-            h2[p, way, n] = go(out_line(p, JB[n], jc), cb[p].at[way, n], net.near(ORDER[p][2], jc))
+            if (n in mine) == arrived:
+                if arrived:
+                    add_line(p, JB[n], jc, [(ca[p], (way, mine.index(n)))])
+                h2[p, way, n] = go(out_line(p, JB[n], jc), cb[p].at[way, n], net.near(ORDER[p][2], jc))
 
     made_twin[steps[0]] = down_twin(*steps[0])
     for i, (p, jc) in enumerate(steps):
@@ -587,20 +570,35 @@
         if jc == 2:
             send_c1(p)
         elif jc != 0:
-            send_c2(p, jc)
-    hb = [[None] * 4 for _ in range(3)]
+            send_c2(p, jc, False)
+    for p in range(3):
+        for jc in (1, 3):
+            send_c2(p, jc, True)
+    halves = (pl.ds(0, 2), pl.ds(2, 2))
+    hb = [[None] * 3 for _ in range(3)]
     for n in range(3):
         for p in range(3):
             for way in range(2):
                 h2[p, way, n].wait_recv()
             add_line(p, JB[n], 0, [(cb[p], (0, n)), (cb[p], (1, n))])
-            hb[p][n] = go(out_line(p, JB[n], 0), bb[p].at[n], net.near(ORDER[p][1], JB[n]))
+            b, c = net.along(ORDER[p][1], JB[n]), net.along(ORDER[p][2], 0)
+            if n == 0:
+                hb[p][0] = []
+                for span, k in zip(halves, (1, 3)):
+                    src = x[p].at[place(p, span, b, c) + (ALL, pl.ds(0, PARTS[p][1]))]
+                    hb[p][0].append(go(src, bb[p].at[0, span], net.near(ORDER[p][1], k)))
+            else:
+                hb[p][0][n - 1].wait_recv()
+                where = place(p, halves[n - 1], b, c) + (ALL, pl.ds(0, PARTS[p][1]))
+                total = x[p][where].astype(jnp.float32) + bb[p][0, halves[n - 1]].astype(jnp.float32)
+                x[p][where] = total.astype(jnp.bfloat16)
+                hb[p][n] = go(out_line(p, JB[n], 0), bb[p].at[n], net.near(ORDER[p][1], JB[n]))
     for p in range(3):
         for way in range(2):
             h2[p, way, 3].wait_recv()
-        for n in range(3):
+        for n in (1, 2):
             hb[p][n].wait_recv()
-        add_line(p, 0, 0, [(cb[p], (0, 3)), (cb[p], (1, 3))] + [(bb[p], (n,)) for n in range(3)])
+        add_line(p, 0, 0, [(cb[p], (0, 3)), (cb[p], (1, 3))] + [(bb[p], (n,)) for n in (1, 2)])
     haa = []
     for p in range(3):
         _, mb, mc = (net.pos[axis] for axis in ORDER[p])
@@ -658,7 +656,6 @@
         + [pltpu.VMEM((3, 4, 16, w), bf) for _, w in PARTS]
         + [pltpu.VMEM((3, 16, w), bf) for _, w in PARTS]
         + [
-            pltpu.VMEM((2, 24, 128), f32),
             pltpu.VMEM((16, 128), f32),
             pltpu.VMEM((2, 16, HALF), f32),
             pltpu.VMEM((4, 4, 576, 128), bf),
@@ -673,8 +670,8 @@
             pltpu.VMEM((4, 4, 16, 256), bf),
             pltpu.VMEM((16, 16, 256), bf),
             pltpu.VMEM((2, 16, HALF), f32),
-            pltpu.VMEM((2, 4, 4, 80, 576), bf),
-            pltpu.VMEM((4, 80, 576), bf),
+            pltpu.VMEM((2, 4, 4, 64, 640), bf),
+            pltpu.VMEM((4, 64, 640), bf),
             pltpu.VMEM((8, 1, 1024), f32),
             pltpu.VMEM((64, 576), f32),
             pltpu.VMEM((16, HALF), f32),
@@ -693,6 +690,28 @@
     )
 
 
+def finish_kernel(mixed, blocks, scales, mixed_out, blocks_out, scales_out):
+    mixed_out[...] = mixed[...]
+    blocks_out[0] = blocks[...]
+    scales_out[...] = jnp.concatenate([scales[i, 0:1, 64:65] for i in range(4)], axis=1)
+
+
+def finish(mixed, blocks, scales):
+    bf = jnp.bfloat16
+    vm = pl.BlockSpec(memory_space=pltpu.VMEM)
+    return pl.pallas_call(
+        finish_kernel,
+        out_shape=(
+            jax.ShapeDtypeStruct((8, WIDE), bf),
+            jax.ShapeDtypeStruct((1, 4, 64, 576), bf),
+            jax.ShapeDtypeStruct((1, 4), bf),
+        ),
+        in_specs=[vm, vm, vm],
+        out_specs=(vm, vm, vm),
+        name="finish",
+    )(mixed, blocks, scales)
+
+
 def body(
     query, cache_pool, block_scale, block_table, lengths, migration, value_up, out_weight, residual, norm_gain,
     expert_ids, gate_weights, expert_owner, w_gate, w_up, w_down,
@@ -701,7 +720,7 @@
         query, cache_pool, block_scale, block_table, lengths, migration, value_up, out_weight, residual,
         norm_gain, expert_ids, gate_weights, expert_owner, w_gate, w_up, w_down,
     )
-    return (mixed, blocks[None], scales[:, 0, 0][None])
+    return finish(mixed, blocks, scales)
 
 
 def solution(mesh):

time: 173 us -> 142 us (0.82)
  Pallas kernels: 167 us -> 141 us
  local copies, waits for them, and re-layouts: 4.6 us -> 0 us
    pallas_call x1, Pallas kernels: 167 us -> 140 us  [layer(): pl.pallas_call(kernel, out_shape=(jax.ShapeDtypeStruct((8, WIDE), bf), ja...]
    unnamed x2 -> x0, local copies, waits for them, and re-layouts: 3.27 us -> none
    pallas_call x0 -> x1, Pallas kernels: none -> 1.78 us  [finish(): pl.pallas_call(finish_kernel, out_shape=(jax.ShapeDtypeStruct((8, WIDE),...]
where the time goes in v4:
time: 142 us
  Pallas kernels  141 us (99%)
    pallas_call x1, Pallas kernels, layer(): pl.pallas_call(kernel, out_shape=(jax.ShapeDtypeStruct((8, WIDE), bf), ja...  140 us

profile of v4, /device:TPU:1, one launch (start us, length us, event | category | flops | bytes accessed | tf_op | source)
XLA Modules:
  0.0 142.1 jit_solution(15483230854185009809)
XLA Ops:
  0.6 139.7 %layer.1 = (bf16[8,7168]{1,0:T(8,128)(2,1)}, bf16[4,64,576]{2,1,0:T(8,128)(2,1)}, bf16[4,16,128]{2,1,0:T(8,128)(2,1)}) custom-call(bf16[32,16,576]{2,1,0:T(8,128)(2,1)} %query.1, bf16[64,576,128]{2,1,0:T(8,128)(2,1)} %bitcast.6, s32[4,32]{1,0:T(4,128)} %bitcast.9, bf16[1,128]{1,0:T(2,128)(2,1)} %bitcast.11, s32[32]{0:T(128)} %lens_s.1, s32[3,16]{1,0:T(4,128)} %bitcast.10, ...), custom_call_target="tpu_custom_call" | custom-call | tf_op jit(solution)/shard_map/layer/pallas_call | solution.py:637
  140.3 1.8 %finish.1 = (bf16[8,7168]{1,0:T(8,128)(2,1)}, bf16[1,4,64,576]{3,2,1,0:T(8,128)(2,1)}, bf16[1,4]{1,0:T(2,128)(2,1)}) custom-call(bf16[8,7168]{1,0:T(8,128)(2,1)} %get-tuple-element.6.mixed, bf16[4,64,576]{2,1,0:T(8,128)(2,1)} %get-tuple-element.7.blocks, bf16[4,16,128]{2,1,0:T(8,128)(2,1)} %get-tuple-element.8.scales), custom_call_target="tpu_custom_call" | custom-call | tf_op jit(solution)/shard_map/finish/pallas_call | solution.py:702

commit v5 on v4

--- a/solution.py
+++ b/solution.py
@@ -76,7 +76,7 @@
     r0, r1, r2, ca0, ca1, ca2, cb0, cb1, cb2, bb0, bb1, bb2, aa0, aa1, aa2,
     both, fin,
     kt, hot, vu, wt, lat, h00, h01, h10, h11, n00, n01, n10, n11, part, px_, rx, sp, gx, res, mg, quarter, lane_scale, row, s16,
-    load, send, recv, recv2, send2,
+    load, send, recv, recv2, send2, recv3, send3,
 ):
     keys_in = (t0, t1, r0, r1)
     net = Links(send, recv)
@@ -301,11 +301,25 @@
             made.wait_recv()
     project(0, twin_heads[0], 1 - core)
 
+    back = []
+
     def shares(half):
         for n in range(2):
             rows = pl.ds(n * 8, 8)
             both = jnp.concatenate([part[half, 0, :, :, rows], part[half, 1, :, :, rows]], axis=2)
             px_[half * 2 + n] = both.astype(bf)
+        for n in range(2):
+            target = half * 2 + n
+            slot = lax.rem(target + 7 - x, 4)
+            made = pltpu.make_async_remote_copy(
+                src_ref=px_.at[target], dst_ref=rx.at[slot], send_sem=send3.at[target], recv_sem=recv3.at[slot],
+                device_id=net.device((target, y, z), core), device_id_type=MESH,
+            )
+            back.append(made)
+
+            @pl.when(target != x)
+            def _():
+                made.start()
 
     shares(0)
     head_finish(1)
@@ -315,11 +329,13 @@
             made.wait_recv()
     project(1, twin_heads[1], 1 - core)
     shares(1)
-    back = [go(px_.at[net.along(0, k)], rx.at[n], net.near(0, k)) for n, k in enumerate((1, 3, 2))]
     mig_spread(0)
     mig_spread(1)
-    for made in back:
-        made.wait_recv()
+    for n in range(3):
+        pltpu.make_async_remote_copy(
+            src_ref=px_.at[0], dst_ref=rx.at[n], send_sem=send3.at[0], recv_sem=recv3.at[n],
+            device_id=net.near(0, 1), device_id_type=MESH,
+        ).wait_recv()
 
     total = px_[x].astype(f32)
     for n in range(3):
@@ -365,6 +381,12 @@
     @pl.when(to_core != core)
     def _():
         away[0].wait_send()
+
+    for target in range(4):
+
+        @pl.when(target != x)
+        def _():
+            back[target].wait_send()
 
     mig_twin(0)
     mig_twin(1)
@@ -397,7 +419,6 @@
         made.wait_recv()
     found = mg[lax.rem(sender, 2), sender // 8, lax.rem(sender // 2, 4)]
     quarter[px] = jnp.where(has_in > 0, found, jnp.zeros_like(found))
-    mx = [go(quarter.at[px], quarter.at[px], net.near(0, k)) for k in (1, 3, 2)]
 
     JS = (0, 1, 3, 2)
     gb = [None] * 3
@@ -457,6 +478,7 @@
                 gf[p][n] = go(src, src, net.near(ORDER[p][2], 3))
             to_twin(p, JS[n], 3)
             to_twin(p, JS[n], 1)
+        for p in range(3):
             if n == 0:
                 multiply(p, x[p], 0, 0)
             if n == 1:
@@ -476,6 +498,7 @@
         for n in range(4):
             gf[p][n].wait_recv()
             to_twin(p, JS[n], 2)
+    for p in range(3):
         multiply(p, x[p], 2, 0)
     for p in range(3):
         for q, jb, kc, made in twins:
@@ -485,12 +508,8 @@
     for made in sent:
         made.wait_send()
     sent.clear()
-
-    for made in mx:
-        made.wait_recv()
-    for i in range(4):
-        blocks_out[i] = quarter[i, :, 0:576]
-        scales_out[i] = quarter[i, 0:16, 512:640]
+    mx = [go(quarter.at[px], quarter.at[px], net.near(0, k)) for k in (1, 3, 2)]
+
     mine = jnp.logical_or(lane == rank, lane == rank + 32)
 
     powers = jnp.logical_and(lane >= 64, lane < 67)
@@ -574,6 +593,11 @@
     for p in range(3):
         for jc in (1, 3):
             send_c2(p, jc, True)
+    for made in mx:
+        made.wait_recv()
+    for i in range(4):
+        blocks_out[i] = quarter[i, :, 0:576]
+        scales_out[i] = quarter[i, 0:16, 512:640]
     halves = (pl.ds(0, 2), pl.ds(2, 2))
     hb = [[None] * 3 for _ in range(3)]
     for n in range(3):
@@ -666,7 +690,7 @@
         ] + head + [
             pltpu.VMEM((2, 2, 4, 4, 16, 256), f32),
             pltpu.VMEM((4, 4, 4, 16, 256), bf),
-            pltpu.VMEM((3, 4, 4, 16, 256), bf),
+            pltpu.VMEM((4, 4, 4, 16, 256), bf),
             pltpu.VMEM((4, 4, 16, 256), bf),
             pltpu.VMEM((16, 16, 256), bf),
             pltpu.VMEM((2, 16, HALF), f32),
@@ -680,6 +704,8 @@
             pltpu.SemaphoreType.DMA((slots,)),
             pltpu.SemaphoreType.DMA((16,)),
             pltpu.SemaphoreType.DMA((16,)),
+            pltpu.SemaphoreType.DMA((4,)),
+            pltpu.SemaphoreType.DMA((4,)),
         ],
         compiler_params=pltpu.CompilerParams(collective_id=1, has_side_effects=True, vmem_limit_bytes=63 * 2**20),
         name="layer",

time: 142 us -> 141 us (level)
  no operation moved by 1% of the time
where the time goes in v5:
time: 141 us
  Pallas kernels  140 us (99%)
    pallas_call x1, Pallas kernels, layer(): pl.pallas_call(kernel, out_shape=(jax.ShapeDtypeStruct((8, WIDE), bf), ja...  138 us

profile of v5, /device:TPU:1, one launch (start us, length us, event | category | flops | bytes accessed | tf_op | source)
XLA Modules:
  0.0 140.7 jit_solution(16744096258356244312)
XLA Ops:
  0.6 138.3 %layer.1 = (bf16[8,7168]{1,0:T(8,128)(2,1)}, bf16[4,64,576]{2,1,0:T(8,128)(2,1)}, bf16[4,16,128]{2,1,0:T(8,128)(2,1)}) custom-call(bf16[32,16,576]{2,1,0:T(8,128)(2,1)} %query.1, bf16[64,576,128]{2,1,0:T(8,128)(2,1)} %bitcast.6, s32[4,32]{1,0:T(4,128)} %bitcast.9, bf16[1,128]{1,0:T(2,128)(2,1)} %bitcast.11, s32[32]{0:T(128)} %lens_s.1, s32[3,16]{1,0:T(4,128)} %bitcast.10, ...), custom_call_target="tpu_custom_call" | custom-call | tf_op jit(solution)/shard_map/layer/pallas_call | solution.py:661
  138.9 1.8 %finish.1 = (bf16[8,7168]{1,0:T(8,128)(2,1)}, bf16[1,4,64,576]{3,2,1,0:T(8,128)(2,1)}, bf16[1,4]{1,0:T(2,128)(2,1)}) custom-call(bf16[8,7168]{1,0:T(8,128)(2,1)} %get-tuple-element.6.mixed, bf16[4,64,576]{2,1,0:T(8,128)(2,1)} %get-tuple-element.7.blocks, bf16[4,16,128]{2,1,0:T(8,128)(2,1)} %get-tuple-element.8.scales), custom_call_target="tpu_custom_call" | custom-call | tf_op jit(solution)/shard_map/finish/pallas_call | solution.py:728
